TPU v7x, 32 devices: a whole 2x2x4 slice. The times are simulated.
32 devices in a mesh: chan: 4 (over x, core), tm: 8 (over z, y).
Axes of the slice: x: 2, y: 2, z: 4, core: 2. Of those that a mesh axis runs over, the one named last changes fastest.
Arguments:
- voltages: bfloat16 [64, 8192, 2, 512], P('tm', 'chan'), may hold values from -8 to 8
- window_stations: int32 [2], replicated, may hold values from 0 to 255
- channel_flags: int32 [8192], replicated, may hold values 0 or 1
Outputs:
- rm_spectrum: float32 [8, 32, 2, 2, 1024], P('tm', 'chan')
- leakage: float32 [2, 256], replicated
All inputs are finite; a program needn't handle non-finite values.
Results may differ from a plain program's by a relative error of at most 0.012.
Values may be sent and summed in bfloat16 or wider, within the bound.
A program may use at most 192 MiB of HBM per device.

v0:
```python
import math

import jax
import jax.numpy as jnp
from jax import lax
from jax.sharding import PartitionSpec as P

CHANNELS = 8192
DEPTH = 1024
ITERATIONS = 3


def phase_table(first_channel, channel_count):
    chan_pos = (first_channel + jnp.arange(channel_count, dtype=jnp.int32)).astype(jnp.float32)
    frequency = 1.0 + (chan_pos + 0.5) / CHANNELS
    lambda_sq = 1.0 / (frequency * frequency)
    depth_grid = (jnp.arange(DEPTH).astype(jnp.float32) - DEPTH // 2) * 2.0
    angles = 2.0 * depth_grid[None, :] * (lambda_sq[:, None] - 0.5)
    return (jnp.cos(angles).astype(jnp.bfloat16), jnp.sin(angles).astype(jnp.bfloat16))


def station_terms(leak_real, leak_imag, fields, station_map, window_map):
    far_real = jnp.sum(station_map * leak_real[None, :], 1)[:, None]
    far_imag = jnp.sum(station_map * leak_imag[None, :], 1)[:, None]
    near_real = jnp.sum(window_map * leak_real[None, :], 1)[None, :]
    near_imag = jnp.sum(window_map * leak_imag[None, :], 1)[None, :]
    row_real = fields[0] - (far_real * fields[2] + far_imag * fields[3])
    row_imag = fields[1] - (far_real * fields[3] - far_imag * fields[2])
    col_real = fields[4] - (near_real * fields[2] + near_imag * fields[3])
    col_imag = -(fields[5] - (near_imag * fields[2] - near_real * fields[3]))
    numer_real = jnp.sum(window_map * jnp.sum(row_real, 0)[:, None], 0) + jnp.sum(
        station_map * jnp.sum(col_real, 1)[:, None], 0
    )
    numer_imag = jnp.sum(window_map * jnp.sum(row_imag, 0)[:, None], 0) + jnp.sum(
        station_map * jnp.sum(col_imag, 1)[:, None], 0
    )
    weight_sum = jnp.sum(window_map * jnp.sum(fields[6], 0)[:, None], 0) + jnp.sum(
        station_map * jnp.sum(fields[7], 1)[:, None], 0
    )
    return (numer_real, numer_imag, weight_sum)


def spectrum_terms(local_vis, first_channel, flag_weights):
    pairs = local_vis.shape[0] // 2
    window = local_vis.shape[2] // 2
    channel_count = local_vis.shape[3]
    six = local_vis.reshape(pairs, 2, 2, window, 2, channel_count)

    def correlation(feed_a, feed_b):
        return six[:, feed_b, :, :, feed_a, :].astype(jnp.float32)

    corr_xx = correlation(0, 0)
    corr_xy = correlation(0, 1)
    corr_yx = correlation(1, 0)
    corr_yy = correlation(1, 1)
    pol_real = 0.5 * (corr_xx[:, 0] - corr_yy[:, 0]) - 0.5 * (corr_xy[:, 1] + corr_yx[:, 1])
    pol_imag = 0.5 * (corr_xx[:, 1] - corr_yy[:, 1]) + 0.5 * (corr_xy[:, 0] + corr_yx[:, 0])
    pol_real = (pol_real * flag_weights).astype(jnp.bfloat16).reshape(pairs * window, channel_count)
    pol_imag = (pol_imag * flag_weights).astype(jnp.bfloat16).reshape(pairs * window, channel_count)

    def conj_sum(left, right):
        real_part = jnp.sum(
            flag_weights * (left[:, 0] * right[:, 0] + left[:, 1] * right[:, 1]), -1
        )
        imag_part = jnp.sum(
            flag_weights * (left[:, 1] * right[:, 0] - left[:, 0] * right[:, 1]), -1
        )
        return (real_part, imag_part)

    cross_real, cross_imag = conj_sum(corr_xy, corr_yy)
    mixed_real, mixed_imag = conj_sum(corr_xx, corr_yy)
    side_real, side_imag = conj_sum(corr_xy, corr_xx)
    power_y = jnp.sum(
        flag_weights * (corr_yy[:, 0] * corr_yy[:, 0] + corr_yy[:, 1] * corr_yy[:, 1]), -1
    )
    power_x = jnp.sum(
        flag_weights * (corr_xx[:, 0] * corr_xx[:, 0] + corr_xx[:, 1] * corr_xx[:, 1]), -1
    )
    baseline_stats = jnp.stack(
        [cross_real, cross_imag, mixed_real, mixed_imag, side_real, side_imag, power_y, power_x], -1
    )
    block_width = math.gcd(channel_count, 1024)

    def add_block(block_id, total):
        offset = block_id * block_width
        cosine, sine_part = phase_table(first_channel + offset, block_width)
        left = jnp.concatenate(
            [
                lax.dynamic_slice_in_dim(pol_real, offset, block_width, 1),
                lax.dynamic_slice_in_dim(pol_imag, offset, block_width, 1),
            ],
            1,
        )
        right = jnp.concatenate(
            [jnp.concatenate([cosine, -sine_part], 1), jnp.concatenate([sine_part, cosine], 1)], 0
        )
        return total + jnp.dot(left, right, preferred_element_type=jnp.float32)

    total = lax.fori_loop(
        0,
        channel_count // block_width,
        add_block,
        jnp.zeros((pairs * window, 2 * DEPTH), jnp.float32),
    )
    return (total.reshape(pairs, window, 2 * DEPTH), baseline_stats)


def per_device(voltages, window_stations, channel_flags):
    tm_size = lax.axis_size("tm")
    inputs = voltages.shape[3]
    stations = inputs // 2
    window = window_stations.shape[0]
    feed_index = (2 * window_stations[:, None] + jnp.arange(2, dtype=jnp.int32)[None, :]).reshape(
        -1
    )
    picked = jnp.take(voltages, feed_index, axis=3)
    blocks = jnp.einsum("tcaw,tcbx->xbawc", picked, voltages, preferred_element_type=jnp.float32)
    summed = lax.psum_scatter(
        jnp.stack([blocks[:, 0, 0] + blocks[:, 1, 1], blocks[:, 0, 1] - blocks[:, 1, 0]], 1).astype(
            jnp.bfloat16
        ),
        "tm",
        scatter_dimension=0,
        tiled=True,
    )
    chan_index = lax.axis_index("chan")
    relaid = lax.all_to_all(summed, "chan", split_axis=0, concat_axis=3, tiled=True)
    spectrum, baseline_stats = spectrum_terms(relaid, 0, channel_flags.astype(jnp.float32))
    own_pairs = spectrum.shape[0]
    total_time = voltages.shape[0] * tm_size
    norm_factor = 1.0 / math.sqrt(CHANNELS * total_time)
    rm_spectrum = (spectrum * norm_factor).reshape(1, own_pairs, window, 2, DEPTH)
    baseline_stats = baseline_stats / CHANNELS
    station_axis = jnp.arange(stations, dtype=jnp.int32)
    window_map = (window_stations[:, None] == station_axis[None, :]).astype(jnp.float32)
    leak_real = jnp.zeros((stations,), jnp.float32)
    leak_imag = jnp.zeros((stations,), jnp.float32)
    first_station = lax.axis_index("tm") * (stations // tm_size) + chan_index * own_pairs
    own_stations = first_station + jnp.arange(own_pairs, dtype=jnp.int32)
    station_map = (own_stations[:, None] == station_axis[None, :]).astype(jnp.float32)
    fields = [baseline_stats[:, :, column] for column in range(8)]
    for iteration in range(ITERATIONS):
        numer_real, numer_imag, weight_sum = station_terms(
            leak_real, leak_imag, fields, station_map, window_map
        )
        numer_real, numer_imag, weight_sum = lax.psum(
            (numer_real, numer_imag, weight_sum), ("chan", "tm")
        )
        leak_real = numer_real / (weight_sum + 1e-06)
        leak_imag = numer_imag / (weight_sum + 1e-06)
    return (rm_spectrum, jnp.stack([leak_real, leak_imag], 0))


def solution(mesh):
    return jax.shard_map(
        per_device,
        mesh=mesh,
        in_specs=(P("tm", "chan", None, None), P(), P()),
        out_specs=(P("tm", "chan", None, None, None), P()),
        check_vma=False,
    )
```

profile of v0, /device:TPU:0, one launch (start us, length us, event | category | flops | bytes accessed | tf_op | source)
XLA Modules:
  0.0 1244.8 jit_solution(1704848731894095129)
XLA Ops:
  8.1 58.0 %copy.112 = bf16[8,2048,2,512]{1,0,2,3:T(8,128)(2,1)} copy(bf16[8,2048,2,512]{3,2,1,0:T(2,128)(2,1)} %param.5) | data formatting | bytes 67108864 | tf_op args[0]
  72.5 44.3 %fusion.20 = f32[512,2,2,4,2048]{0,3,1,2,4:T(4,128)} fusion(bf16[8,2048,2,4,1]{0,3,4,2,1:T(4,128)(2,1)} %copy.142, bf16[8,2048,2,512,1]{3,2,1,0,4:T(2,128)(2,1)} %bitcast.190), kind=kOutput, calls=%fused_computation.25 | convolution fusion | flops 268435456 | bytes 100925440 | tf_op jit(solution)/shard_map/tcaw,tcbx->xbawc/dot_general | solution.py:117
  116.8 13.2 %fusion.26 = bf16[512,1,4,2048]{0,2,3,1:T(4,128)(2,1)S(1)} fusion(f32[512,2,2,4,2048]{0,3,1,2,4:T(4,128)} %fusion.20), kind=kLoop, calls=%fused_computation.33 | loop fusion | flops 8388608 | bytes 41943040 | tf_op jit(solution)/shard_map/add | solution.py:119
  130.0 13.2 %fusion.27 = bf16[512,1,4,2048]{0,2,3,1:T(4,128)(2,1)S(1)} fusion(f32[512,2,2,4,2048]{0,3,1,2,4:T(4,128)} %fusion.20), kind=kLoop, calls=%fused_computation.34 | loop fusion | flops 8388608 | bytes 41943040 | tf_op jit(solution)/shard_map/sub | solution.py:119
  143.1 13.9 %pad_maximum_fusion = bf16[512,2,4,2048]{0,2,3,1:T(4,128)(2,1)} fusion(bf16[512,1,4,2048]{0,2,3,1:T(4,128)(2,1)S(1)} %fusion.27, bf16[512,1,4,2048]{0,2,3,1:T(4,128)(2,1)S(1)} %fusion.26), kind=kLoop, calls=%fused_computation.32 | loop fusion | flops 8388608 | bytes 33554432 | tf_op jit(solution)/shard_map/stack | solution.py:119
  157.0 36.9 %copy.117 = bf16[512,2,4,2048]{3,2,1,0:T(4,128)(2,1)} copy(bf16[512,2,4,2048]{0,2,3,1:T(4,128)(2,1)} %pad_maximum_fusion) | data formatting | bytes 33554432 | tf_op jit(solution)/shard_map/stack | solution.py:119
  195.8 510.3 %all-reduce.6.cloned.1.call-done = bf16[512,2,4,2048]{3,2,1,0:T(4,128)(2,1)} async-done(((bf16[512,2,4,2048]{3,2,1,0:T(4,128)(2,1)}), bf16[512,2,4,2048]{3,2,1,0:T(4,128)(2,1)}) %all-reduce.6.cloned.1.call-update) | async-done | bytes 16777232
  714.6 25.4 %all-to-all-done = bf16[64,2,4,2048]{3,2,1,0:T(4,128)(2,1)S(1)} async-done(((bf16[64,2,4,2048]{3,2,1,0:T(4,128)(2,1)}), bf16[64,2,4,2048]{3,2,1,0:T(4,128)(2,1)S(1)}, u32[]{:S(2)}, u32[]{:S(2)}) %all-to-all-start) | async-done | bytes 2097184 | tf_op jit(solution)/shard_map/all_to_all | solution.py:127
  757.4 38.5 %all-reduce.3 = (f32[256]{0:T(256)S(1)}, f32[256]{0:T(256)S(1)}, f32[256]{0:T(256)S(1)}) all-reduce(f32[256]{0:T(256)S(1)} %add.315, f32[256]{0:T(256)S(1)} %add.316, f32[256]{0:T(256)S(1)} %add.318), channel_id=1, replica_groups=mesh['chan'=4,'tm'=8] {'chan','tm'}, use_global_device_ids=true, to_apply=%region_15.16 | all-reduce | flops 768 | bytes 6144 | tf_op jit(solution)/shard_map/psum | solution.py:146
  796.6 41.1 %all-reduce.2 = (f32[256]{0:T(256)S(1)}, f32[256]{0:T(256)S(1)}) all-reduce(f32[256]{0:T(256)S(1)} %add.321, f32[256]{0:T(256)S(1)} %add.322), channel_id=1, replica_groups=mesh['chan'=4,'tm'=8] {'chan','tm'}, use_global_device_ids=true, to_apply=%region_34.35 | all-reduce | flops 512 | bytes 4096 | tf_op jit(solution)/shard_map/psum | solution.py:146
  843.2 353.9 %while.16 = (s32[]{:T(128)}, f32[16,2048]{1,0:T(8,128)S(1)}, bf16[16,8192]{1,0:T(8,128)(2,1)S(1)}, bf16[16,8192]{1,0:T(8,128)(2,1)S(1)}, s32[]{:T(128)}, /*index=5*/s32[]{:T(128)}, s32[]{:T(128)}, s32[]{:T(128)}) while((s32[]{:T(128)}, f32[16,2048]{1,0:T(8,128)S(1)}, bf16[16,8192]{1,0:T(8,128)(2,1)S(1)}, ...), condition=%wide.region_2.3_spmd.clone, body=%wide.region_1.2_spmd.clone.sunk | while | flops 176368640 | bytes 13066389 | solution.py:99
  843.2 16.9 %fusion.59 = (bf16[1024,1024]{1,0:T(8,128)(2,1)S(1)}, bf16[1024,1024]{1,0:T(8,128)(2,1)}) fusion(f32[1024]{0:T(1024)S(1)} %get-tuple-element.252, f32[1024]{0:T(1024)S(1)} %get-tuple-element.253), kind=kLoop, calls=%fused_computation.12.clone.2 | loop fusion | flops 3145728 | bytes 4202496 | tf_op jit(solution)/shard_map/while/body/eval_jaxpr/convert_element_type | solution.py:19
  860.1 15.1 %fusion.60 = bf16[1024,1024]{1,0:T(8,128)(2,1)} fusion(f32[1024]{0:T(1024)S(1)} %get-tuple-element.252, f32[1024]{0:T(1024)S(1)} %get-tuple-element.253), kind=kLoop, calls=%fused_computation.14.clone.1 | loop fusion | flops 5242880 | bytes 2105344 | tf_op jit(solution)/shard_map/while/body/eval_jaxpr/neg | solution.py:95
  875.2 12.2 fusion.61
  887.4 16.9 %fusion.59 = (bf16[1024,1024]{1,0:T(8,128)(2,1)S(1)}, bf16[1024,1024]{1,0:T(8,128)(2,1)}) fusion(f32[1024]{0:T(1024)S(1)} %get-tuple-element.252, f32[1024]{0:T(1024)S(1)} %get-tuple-element.253), kind=kLoop, calls=%fused_computation.12.clone.2 | loop fusion | flops 3145728 | bytes 4202496 | tf_op jit(solution)/shard_map/while/body/eval_jaxpr/convert_element_type | solution.py:19
  904.4 15.1 %fusion.60 = bf16[1024,1024]{1,0:T(8,128)(2,1)} fusion(f32[1024]{0:T(1024)S(1)} %get-tuple-element.252, f32[1024]{0:T(1024)S(1)} %get-tuple-element.253), kind=kLoop, calls=%fused_computation.14.clone.1 | loop fusion | flops 5242880 | bytes 2105344 | tf_op jit(solution)/shard_map/while/body/eval_jaxpr/neg | solution.py:95
  919.5 12.2 fusion.61
  931.7 16.9 %fusion.59 = (bf16[1024,1024]{1,0:T(8,128)(2,1)S(1)}, bf16[1024,1024]{1,0:T(8,128)(2,1)}) fusion(f32[1024]{0:T(1024)S(1)} %get-tuple-element.252, f32[1024]{0:T(1024)S(1)} %get-tuple-element.253), kind=kLoop, calls=%fused_computation.12.clone.2 | loop fusion | flops 3145728 | bytes 4202496 | tf_op jit(solution)/shard_map/while/body/eval_jaxpr/convert_element_type | solution.py:19
  948.6 15.1 %fusion.60 = bf16[1024,1024]{1,0:T(8,128)(2,1)} fusion(f32[1024]{0:T(1024)S(1)} %get-tuple-element.252, f32[1024]{0:T(1024)S(1)} %get-tuple-element.253), kind=kLoop, calls=%fused_computation.14.clone.1 | loop fusion | flops 5242880 | bytes 2105344 | tf_op jit(solution)/shard_map/while/body/eval_jaxpr/neg | solution.py:95
  975.9 16.9 %fusion.59 = (bf16[1024,1024]{1,0:T(8,128)(2,1)S(1)}, bf16[1024,1024]{1,0:T(8,128)(2,1)}) fusion(f32[1024]{0:T(1024)S(1)} %get-tuple-element.252, f32[1024]{0:T(1024)S(1)} %get-tuple-element.253), kind=kLoop, calls=%fused_computation.12.clone.2 | loop fusion | flops 3145728 | bytes 4202496 | tf_op jit(solution)/shard_map/while/body/eval_jaxpr/convert_element_type | solution.py:19
  992.8 15.1 %fusion.60 = bf16[1024,1024]{1,0:T(8,128)(2,1)} fusion(f32[1024]{0:T(1024)S(1)} %get-tuple-element.252, f32[1024]{0:T(1024)S(1)} %get-tuple-element.253), kind=kLoop, calls=%fused_computation.14.clone.1 | loop fusion | flops 5242880 | bytes 2105344 | tf_op jit(solution)/shard_map/while/body/eval_jaxpr/neg | solution.py:95
  1007.9 12.2 fusion.61
  1020.1 16.9 %fusion.59 = (bf16[1024,1024]{1,0:T(8,128)(2,1)S(1)}, bf16[1024,1024]{1,0:T(8,128)(2,1)}) fusion(f32[1024]{0:T(1024)S(1)} %get-tuple-element.252, f32[1024]{0:T(1024)S(1)} %get-tuple-element.253), kind=kLoop, calls=%fused_computation.12.clone.2 | loop fusion | flops 3145728 | bytes 4202496 | tf_op jit(solution)/shard_map/while/body/eval_jaxpr/convert_element_type | solution.py:19
  1037.1 15.1 %fusion.60 = bf16[1024,1024]{1,0:T(8,128)(2,1)} fusion(f32[1024]{0:T(1024)S(1)} %get-tuple-element.252, f32[1024]{0:T(1024)S(1)} %get-tuple-element.253), kind=kLoop, calls=%fused_computation.14.clone.1 | loop fusion | flops 5242880 | bytes 2105344 | tf_op jit(solution)/shard_map/while/body/eval_jaxpr/neg | solution.py:95
  1052.1 12.2 fusion.61
  1064.4 16.9 %fusion.59 = (bf16[1024,1024]{1,0:T(8,128)(2,1)S(1)}, bf16[1024,1024]{1,0:T(8,128)(2,1)}) fusion(f32[1024]{0:T(1024)S(1)} %get-tuple-element.252, f32[1024]{0:T(1024)S(1)} %get-tuple-element.253), kind=kLoop, calls=%fused_computation.12.clone.2 | loop fusion | flops 3145728 | bytes 4202496 | tf_op jit(solution)/shard_map/while/body/eval_jaxpr/convert_element_type | solution.py:19
  1081.3 15.1 %fusion.60 = bf16[1024,1024]{1,0:T(8,128)(2,1)} fusion(f32[1024]{0:T(1024)S(1)} %get-tuple-element.252, f32[1024]{0:T(1024)S(1)} %get-tuple-element.253), kind=kLoop, calls=%fused_computation.14.clone.1 | loop fusion | flops 5242880 | bytes 2105344 | tf_op jit(solution)/shard_map/while/body/eval_jaxpr/neg | solution.py:95
  1108.6 16.9 %fusion.59 = (bf16[1024,1024]{1,0:T(8,128)(2,1)S(1)}, bf16[1024,1024]{1,0:T(8,128)(2,1)}) fusion(f32[1024]{0:T(1024)S(1)} %get-tuple-element.252, f32[1024]{0:T(1024)S(1)} %get-tuple-element.253), kind=kLoop, calls=%fused_computation.12.clone.2 | loop fusion | flops 3145728 | bytes 4202496 | tf_op jit(solution)/shard_map/while/body/eval_jaxpr/convert_element_type | solution.py:19
  1125.5 15.1 %fusion.60 = bf16[1024,1024]{1,0:T(8,128)(2,1)} fusion(f32[1024]{0:T(1024)S(1)} %get-tuple-element.252, f32[1024]{0:T(1024)S(1)} %get-tuple-element.253), kind=kLoop, calls=%fused_computation.14.clone.1 | loop fusion | flops 5242880 | bytes 2105344 | tf_op jit(solution)/shard_map/while/body/eval_jaxpr/neg | solution.py:95
  1152.8 16.9 %fusion.59 = (bf16[1024,1024]{1,0:T(8,128)(2,1)S(1)}, bf16[1024,1024]{1,0:T(8,128)(2,1)}) fusion(f32[1024]{0:T(1024)S(1)} %get-tuple-element.252, f32[1024]{0:T(1024)S(1)} %get-tuple-element.253), kind=kLoop, calls=%fused_computation.12.clone.2 | loop fusion | flops 3145728 | bytes 4202496 | tf_op jit(solution)/shard_map/while/body/eval_jaxpr/convert_element_type | solution.py:19
  1169.7 15.1 %fusion.60 = bf16[1024,1024]{1,0:T(8,128)(2,1)} fusion(f32[1024]{0:T(1024)S(1)} %get-tuple-element.252, f32[1024]{0:T(1024)S(1)} %get-tuple-element.253), kind=kLoop, calls=%fused_computation.14.clone.1 | loop fusion | flops 5242880 | bytes 2105344 | tf_op jit(solution)/shard_map/while/body/eval_jaxpr/neg | solution.py:95
  1198.0 39.3 %all-reduce.1 = (f32[256]{0:T(256)S(1)}, f32[256]{0:T(256)S(1)}) all-reduce(f32[256]{0:T(256)S(1)} %add.326, f32[256]{0:T(256)S(1)} %add.325), channel_id=1, replica_groups=mesh['chan'=4,'tm'=8] {'chan','tm'}, use_global_device_ids=true, to_apply=%region_53.54 | all-reduce | flops 512 | bytes 4096 | tf_op jit(solution)/shard_map/psum | solution.py:146
  (98 shorter events, 90.9 us)
Async XLA Ops:
  7.2 698.9 %all-reduce.6.cloned.1.call-start = ((), (), s32[]{:S(2)}) async-start(), calls=%async_computation.1 | async-start | bytes 33554432
  193.9 0.7 copy-start.2
  194.0 520.6 %copy-start = (s32[8192]{0:T(1024)S(1)}, s32[8192]{0:T(1024)}, u32[]{:S(2)}) copy-start(s32[8192]{0:T(1024)} %param.7) | copy-start | bytes 98308
  710.8 29.3 %all-to-all-start = ((bf16[64,2,4,2048]{3,2,1,0:T(4,128)(2,1)}), bf16[64,2,4,2048]{3,2,1,0:T(4,128)(2,1)S(1)}, u32[]{:S(2)}, u32[]{:S(2)}) async-start(bf16[64,2,4,2048]{3,2,1,0:T(4,128)(2,1)} %constant_dynamic-slice_fusion.2), calls=%async_computation | async-start | bytes 4194304 | tf_op jit(solution)/shard_map/all_to_all | solution.py:127
  747.9 9.3 copy-start.1
Sparse Core Ops, SparseCore 0:
  194.1 511.9 all-reduce.5
where the time goes:
time: 1250 us; the launch traced here: 1240 us
  waiting for transfers between devices  536 us (43%)
  other arithmetic  306 us (24%)
  matrix products  142 us (11%)
  local copies, waits for them, and re-layouts  123 us (10%)
  blocking collectives  119 us (10%)
  between operations  15 us (1%)
    unnamed x2, waiting for transfers between devices  510 us
    convert_element_type x8, other arithmetic, phase_table(): jnp.sin(angles).astype(jnp.bfloat16)  135 us
    neg x8, other arithmetic, add_block(): -sine_part  121 us
    psum x3, blocking collectives, per_device(): lax.psum((numer_real, numer_imag, weight_sum), ('chan', 'tm'))  119 us
    dot_general x8, matrix products, add_block(): return total + jnp.dot(left, right, preferred_element_type=jnp.float32)  97.5 us
    unnamed x16, local copies, waits for them, and re-layouts  64 us
    dot_general x1, matrix products, per_device(): jnp.einsum('tcaw,tcbx->xbawc', picked, voltages, preferred_element_type=j...  44.3 us
    another operation x1, local copies, waits for them, and re-layouts, per_device(): jnp.stack([blocks[:, 0, 0] + blocks[:, 1, 1], blocks[:, 0, 1] - blocks[:,...  36.9 us
  transfers between devices with their start and end apart: 2, of which 2 were waited for; matrix products, arithmetic and copies ran while one was open for 0% of the time, Pallas kernels for 0%

commit v1 on v0

v1 whole, which is shorter than its diff:
```python
import math

import jax
import jax.numpy as jnp
from jax import lax
from jax.experimental import pallas as pl
from jax.experimental.pallas import tpu as pltpu
from jax.sharding import PartitionSpec as P

CHANNELS = 8192
DEPTH = 1024
ITERATIONS = 3
GROUP = 16
LANES = 128
NUM_Z = 4
CORES = 2
CHUNKS = 4
F32 = jnp.float32
BF16 = jnp.bfloat16


def correlate_kernel(scalars, x_ref, vis_ref, pol_ref):
    times, _, parts, inputs = x_ref.shape
    depth = times * GROUP * parts
    columns = 8 * GROUP
    row = lax.broadcasted_iota(jnp.int32, (depth, columns), 0)
    col = lax.broadcasted_iota(jnp.int32, (depth, columns), 1)
    same_channel = lax.rem(lax.div(row, parts), GROUP) == lax.rem(col, GROUP)
    is_real_row = lax.rem(row, parts) == 0
    is_real_col = col < 4 * GROUP
    feed = lax.rem(lax.div(lax.broadcasted_iota(jnp.int32, (inputs, columns), 1), GROUP), 4)
    station = jnp.where(feed < 2, scalars[1], scalars[2])
    pick = (
        lax.broadcasted_iota(jnp.int32, (inputs, columns), 0) == 2 * station + lax.rem(feed, 2)
    ).astype(F32).astype(BF16)
    first_feed = lax.rem(lax.broadcasted_iota(jnp.int32, (GROUP, inputs), 1), 2) == 0
    pair_sum = (
        lax.div(lax.broadcasted_iota(jnp.int32, (inputs, inputs // 2), 0), 2)
        == lax.broadcasted_iota(jnp.int32, (inputs, inputs // 2), 1)
    ).astype(F32).astype(BF16)

    def body(step, carry):
        start = pl.multiple_of(step * GROUP, GROUP)
        here = pl.ds(start, GROUP)
        x = x_ref[:, here, :, :].reshape(depth, inputs)
        picked = jnp.dot(x, pick, preferred_element_type=F32)
        swapped = jnp.where(
            is_real_row, pltpu.roll(picked, depth - 1, 0), -pltpu.roll(picked, 1, 0)
        )
        left = jnp.where(same_channel, jnp.where(is_real_col, picked, swapped), 0.0).astype(BF16)
        out = lax.dot_general(
            left, x, (((0,), (0,)), ((), ())), preferred_element_type=F32
        )

        def rows(part, window, feed_a):
            first = (part * 4 + 2 * window + feed_a) * GROUP
            return out[first : first + GROUP]

        for window in range(2):
            for part in range(2):
                vis_ref[2 * window + part, here, :] = rows(part, window, 0).astype(BF16)
        for part in range(2):
            vis_ref[4 + part, here, :] = jnp.where(
                first_feed, pltpu.roll(rows(part, 1, 1), inputs - 1, 1), rows(part, 0, 1)
            ).astype(BF16)
        pols = []
        for window in range(2):
            x_real, x_imag = rows(0, window, 0), rows(1, window, 0)
            y_real, y_imag = rows(0, window, 1), rows(1, window, 1)
            pols.append(jnp.where(first_feed, x_real - y_imag, -(y_real + x_imag)))
            pols.append(jnp.where(first_feed, x_imag + y_real, x_real - y_imag))
        pol = jnp.concatenate([(0.5 * value).astype(BF16) for value in pols], 0)
        summed = jnp.dot(pol, pair_sum, preferred_element_type=F32).astype(BF16)
        for index in range(4):
            pol_ref[index, here, :] = summed[index * GROUP : (index + 1) * GROUP]
        return carry

    lax.fori_loop(0, x_ref.shape[1] // GROUP, body, 0, unroll=2)


def correlate(voltages, window_stations, first, count):
    times, _, parts, inputs = voltages.shape
    block = math.gcd(count, 64)
    scalars = jnp.concatenate(
        [jnp.reshape(lax.div(first, block), (1,)), window_stations]
    ).astype(jnp.int32)
    return pl.pallas_call(
        correlate_kernel,
        grid_spec=pltpu.PrefetchScalarGridSpec(
            num_scalar_prefetch=1,
            grid=(count // block,),
            in_specs=[pl.BlockSpec((times, block, parts, inputs), lambda i, s: (0, s[0] + i, 0, 0))],
            out_specs=[
                pl.BlockSpec((6, block, inputs), lambda i, s: (0, i, 0)),
                pl.BlockSpec((4, block, inputs // 2), lambda i, s: (0, i, 0)),
            ],
        ),
        out_shape=[
            jax.ShapeDtypeStruct((6, count, inputs), BF16),
            jax.ShapeDtypeStruct((4, count, inputs // 2), BF16),
        ],
        compiler_params=pltpu.CompilerParams(vmem_limit_bytes=40 << 20),
        cost_estimate=pl.CostEstimate(
            flops=count * 16 * 2 * 512 * 256, bytes_accessed=count * 16 * 1024 * 2, transcendentals=0
        ),
        name="correlate",
    )(scalars, voltages)


def transform_kernel(pol_ref, fine_ref, coarse_ref, out_ref, table):
    @pl.when(pl.program_id(0) == 0)
    def _():
        out_ref[...] = jnp.zeros_like(out_ref)

    fine_cos, fine_sin = fine_ref[0], fine_ref[1]
    blocks = DEPTH // LANES
    for block in range(blocks):
        cos = coarse_ref[:, block : block + 1]
        sin = coarse_ref[:, blocks + block : blocks + block + 1]
        table[:, block * LANES : (block + 1) * LANES] = (cos * fine_cos - sin * fine_sin).astype(BF16)
        table[:, DEPTH + block * LANES : DEPTH + (block + 1) * LANES] = (
            sin * fine_cos + cos * fine_sin
        ).astype(BF16)

    def dot(left, right):
        return lax.dot_general(left, right, (((0,), (0,)), ((), ())), preferred_element_type=F32)

    width = 256
    for first in range(0, DEPTH, width):
        cosine = table[:, first : first + width]
        sine = table[:, DEPTH + first : DEPTH + first + width]
        for window in range(2):
            real, imag = pol_ref[2 * window], pol_ref[2 * window + 1]
            out_ref[:, window, 0, first : first + width] += dot(real, cosine) + dot(imag, sine)
            out_ref[:, window, 1, first : first + width] += dot(imag, cosine) - dot(real, sine)


def transform(pol, fine, coarse):
    _, count, stations = pol.shape
    block = math.gcd(count, 256)
    out = pl.pallas_call(
        lambda p, f, c, o, t: transform_kernel(
            p, f, c, o, t
        ),
        grid=(count // block,),
        in_specs=[
            pl.BlockSpec((4, block, stations), lambda i: (0, i, 0)),
            pl.BlockSpec((2, block, LANES), lambda i: (0, i, 0)),
            pl.BlockSpec((block, coarse.shape[1]), lambda i: (i, 0)),
        ],
        out_specs=pl.BlockSpec((stations, 2, 2, DEPTH), lambda i: (0, 0, 0, 0)),
        out_shape=jax.ShapeDtypeStruct((stations, 2, 2, DEPTH), F32),
        scratch_shapes=[pltpu.VMEM((block, 2 * DEPTH), BF16)],
        compiler_params=pltpu.CompilerParams(vmem_limit_bytes=40 << 20),
        cost_estimate=pl.CostEstimate(
            flops=2 * count * 4 * stations * 2 * DEPTH, bytes_accessed=16 << 20, transcendentals=0
        ),
        name="transform",
    )(pol, fine, coarse)
    return out


def tables(channels, flag_weights):
    frequency = 1.0 + (channels.astype(F32) + 0.5) / CHANNELS
    scaled = 2.0 * (1.0 / (frequency * frequency) - 0.5)
    fine_depth = 2.0 * jnp.arange(LANES, dtype=jnp.int32).astype(F32)
    fine_angle = scaled[:, None] * fine_depth[None, :]
    fine = jnp.stack([jnp.cos(fine_angle), jnp.sin(fine_angle)], 0)
    coarse_depth = 2.0 * (jnp.arange(DEPTH // LANES, dtype=jnp.int32) * LANES - DEPTH // 2).astype(F32)
    coarse_angle = coarse_depth[:, None] * scaled[None, :]
    coarse = jnp.concatenate([jnp.cos(coarse_angle), jnp.sin(coarse_angle)], 0) * flag_weights[None, :]
    return fine, coarse.T


def statistics_kernel(vis_ref, flag_ref, out_ref):
    inputs = vis_ref.shape[2]

    def body(step, total):
        here = pl.ds(pl.multiple_of(step * GROUP, GROUP), GROUP)
        flag = flag_ref[here, :]
        values = [vis_ref[index, here, :].astype(F32) for index in range(6)]
        found = []
        for window in range(2):
            xx = values[2 * window : 2 * window + 2]
            xy = [pltpu.roll(value, inputs - 1, 1) for value in xx]
            yy = values[4:6]
            if window == 0:
                yy = [pltpu.roll(value, inputs - 1, 1) for value in yy]
            for left, right in ((xy, yy), (xx, yy), (xy, xx)):
                found.append(left[0] * right[0] + left[1] * right[1])
                found.append(left[1] * right[0] - left[0] * right[1])
            found.append(yy[0] * yy[0] + yy[1] * yy[1])
            found.append(xx[0] * xx[0] + xx[1] * xx[1])
        rows = [jnp.sum(flag * value, 0, keepdims=True) for value in found]
        return total + jnp.concatenate(rows, 0)

    out_ref[...] = lax.fori_loop(
        0, vis_ref.shape[1] // GROUP, body, jnp.zeros(out_ref.shape, F32)
    )


def statistics(vis, flags):
    return pl.pallas_call(
        statistics_kernel,
        out_shape=jax.ShapeDtypeStruct((16, vis.shape[2]), F32),
        compiler_params=pltpu.CompilerParams(vmem_limit_bytes=40 << 20),
        name="statistics",
    )(vis, flags)


def fit_kernel(stations_ref, stats_ref, out_ref):
    count = stats_ref.shape[1]
    lane = lax.broadcasted_iota(jnp.int32, (1, count), 1)
    chosen = [(lane == stations_ref[window]).astype(F32) for window in range(2)]

    def total(value):
        return jnp.sum(value, 1, keepdims=True)

    def field(window, index):
        return stats_ref[8 * window + index : 8 * window + index + 1, :]

    weights = jnp.zeros((1, count), F32)
    for window in range(2):
        weights += chosen[window] * total(field(window, 6)) + field(window, 7)
    weights += 1e-6
    real = jnp.zeros((1, count), F32)
    imag = jnp.zeros((1, count), F32)
    for _ in range(ITERATIONS):
        numer_real = jnp.zeros((1, count), F32)
        numer_imag = jnp.zeros((1, count), F32)
        for window in range(2):
            cross_r, cross_i, mixed_r, mixed_i, side_r, side_i = [
                field(window, index) for index in range(6)
            ]
            near_real = total(chosen[window] * real)
            near_imag = total(chosen[window] * imag)
            row_real = cross_r - (real * mixed_r + imag * mixed_i)
            row_imag = cross_i - (real * mixed_i - imag * mixed_r)
            col_real = side_r - (near_real * mixed_r + near_imag * mixed_i)
            col_imag = -(side_i - (near_imag * mixed_r - near_real * mixed_i))
            numer_real += chosen[window] * total(row_real) + col_real
            numer_imag += chosen[window] * total(row_imag) + col_imag
        real = numer_real / weights
        imag = numer_imag / weights
    out_ref[0:1, :] = real
    out_ref[1:2, :] = imag


def fit(stats, window_stations):
    return pl.pallas_call(
        fit_kernel,
        in_specs=[
            pl.BlockSpec(memory_space=pltpu.SMEM),
            pl.BlockSpec(memory_space=pltpu.VMEM),
        ],
        out_shape=jax.ShapeDtypeStruct((2, stats.shape[1]), F32),
        name="fit",
    )(window_stations, stats)


def add(left, right):
    return (left.astype(F32) + right.astype(F32)).astype(BF16)


def ring_sum(block_of, place, size, axis, pairs):
    running = block_of(lax.rem(place + size - 1, size))
    for step in range(1, size):
        running = lax.ppermute(running, axis, pairs)
        running = add(running, block_of(lax.rem(place + 2 * size - 1 - step, size)))
    return running


def per_device(voltages, window_stations, channel_flags):
    tm_size = lax.axis_size("tm")
    chan_size = lax.axis_size("chan")
    times, local, _, inputs = voltages.shape
    stations = inputs // 2
    tm, chan = lax.axis_index("tm"), lax.axis_index("chan")
    num_z, num_y = NUM_Z, tm_size // NUM_Z
    place_z, place_y = lax.div(tm, num_y), lax.rem(tm, num_y)
    num_x, place_x, core = chan_size // CORES, lax.div(chan, CORES), lax.rem(chan, CORES)
    y_pairs = [
        (z * num_y + y, z * num_y + (y + 1) % num_y) for z in range(num_z) for y in range(num_y)
    ]
    z_pairs = [
        (z * num_y + y, ((z + 1) % num_z) * num_y + y) for z in range(num_z) for y in range(num_y)
    ]
    x_pairs = [(x * CORES + c, ((x + 1) % num_x) * CORES + c) for x in range(num_x) for c in range(CORES)]
    core_pairs = [(x * CORES + c, x * CORES + (c + 1) % CORES) for x in range(num_x) for c in range(CORES)]

    per_y = local // num_y
    per_chunk = per_y // CHUNKS
    per_z = per_chunk // num_z
    order = [lax.rem(place_y + 2 * num_y - 1 - step, num_y) for step in range(num_y)]
    vis, pols, visited = {}, [], []
    for step, y_block in enumerate(order):
        for chunk in range(CHUNKS):
            first = y_block * per_y + chunk * per_chunk
            vis[step, chunk], pol = correlate(voltages, window_stations, first, per_chunk)
            pols.append(pol)
            visited.append(chan * local + first + jnp.arange(per_chunk, dtype=jnp.int32))
    weights = channel_flags.astype(F32)

    finished = []
    for chunk in range(CHUNKS):
        running = vis[0, chunk]
        for step in range(1, num_y):
            running = add(lax.ppermute(running, "tm", y_pairs), vis[step, chunk])
        parts = running.reshape(6, num_z, per_z, inputs)

        def z_block(index, parts=parts):
            return lax.dynamic_index_in_dim(parts, index, 1, keepdims=False)

        finished.append(ring_sum(z_block, place_z, num_z, "tm", z_pairs))
    own_vis = jnp.concatenate(finished, 1)
    own_flags = lax.dynamic_slice(
        weights.reshape(chan_size, num_y, CHUNKS, num_z, per_z),
        (chan, place_y, 0, place_z, 0),
        (1, 1, CHUNKS, 1, per_z),
    ).reshape(-1, 1)

    by_y = lax.dynamic_slice_in_dim(weights, chan * local, local, 0).reshape(num_y, per_y)
    local_flags = jnp.concatenate(
        [lax.dynamic_index_in_dim(by_y, y_block, 0, keepdims=False) for y_block in order]
    )
    fine, coarse = tables(jnp.concatenate(visited), local_flags)
    spectrum = transform(jnp.concatenate(pols, 1), fine, coarse)
    own = stations // (tm_size * chan_size)
    cube = spectrum.astype(BF16).reshape(num_z, num_y, num_x, CORES, own, 2, 2, DEPTH)
    for axis, pairs, place, size, dim in (
        ("chan", core_pairs, core, CORES, 3),
        ("chan", x_pairs, place_x, num_x, 2),
        ("tm", y_pairs, place_y, num_y, 1),
        ("tm", z_pairs, place_z, num_z, 0),
    ):
        def block_of(index, cube=cube, dim=dim):
            return lax.dynamic_index_in_dim(cube, index, dim, keepdims=False)

        cube = ring_sum(block_of, place, size, axis, pairs)
    norm_factor = 1.0 / math.sqrt(CHANNELS * times * tm_size)
    rm_spectrum = (cube.astype(F32) * norm_factor).reshape(1, own, 2, 2, DEPTH)

    stats = statistics(own_vis, own_flags).reshape(16, stations, 2)[:, :, 0]
    stats = lax.psum(stats, ("chan", "tm")) / CHANNELS
    return (rm_spectrum, fit(stats, window_stations))


def solution(mesh):
    return jax.shard_map(
        per_device,
        mesh=mesh,
        in_specs=(P("tm", "chan", None, None), P(), P()),
        out_specs=(P("tm", "chan", None, None, None), P()),
        check_vma=False,
    )
```

time: 1250 us -> 438 us (0.35)
  waiting for transfers between devices: 536 us -> 191 us
  other arithmetic: 306 us -> 25.6 us
  matrix products: 142 us -> 0 us
  Pallas kernels: 0 us -> 126 us
  local copies, waits for them, and re-layouts: 123 us -> 30.2 us
  blocking collectives: 119 us -> 37.9 us
  starting transfers between devices: 3.83 us -> 25 us
  between operations: 15 us -> 1.34 us
    unnamed x2 -> x0, waiting for transfers between devices: 510 us -> none
    ppermute x0 -> x22, waiting for transfers between devices: none -> 191 us  [the longest x18 120 us: ring_sum(): running = lax.ppermute(running, axis, pairs)]
    dot_general x9 -> x0, matrix products: 142 us -> none  [the longest x8 97.5 us: add_block(): return total + jnp.dot(left, right, preferred_element_type=jnp.float32)]
    pallas_call x0 -> x11, Pallas kernels: none -> 126 us  [the longest x8 86.8 us: correlate(): pl.pallas_call(correlate_kernel, grid_spec=pltpu.PrefetchScalarGridSpec(n...]
    convert_element_type x13 -> x23, other arithmetic: 139 us -> 17.2 us  [the longest x21 13.9 us: add(): return (left.astype(F32) + right.astype(F32)).astype(BF16)]
    neg x11 -> x0, other arithmetic: 121 us -> none  [the longest x8 121 us: add_block(): -sine_part]
    psum x3 -> x1, blocking collectives: 119 us -> 37.9 us  [per_device(): stats = lax.psum(stats, ('chan', 'tm')) / CHANNELS]
    unnamed x16 -> x54, local copies, waits for them, and re-layouts: 64 us -> 19.5 us
  transfers between devices with their start and end apart: 2 -> 22, of which waited for: 2 -> 18; matrix products, arithmetic and copies ran while one was open for 0% -> 4% of each run, Pallas kernels for 0% -> 0%
where the time goes in v1:
time: 438 us; the launch traced here: 437 us
  waiting for transfers between devices  191 us (44%)
  Pallas kernels  126 us (29%)
  blocking collectives  37.9 us (9%)
  local copies, waits for them, and re-layouts  30.2 us (7%)
  other arithmetic  25.6 us (6%)
  starting transfers between devices  25 us (6%)
    ppermute x18, waiting for transfers between devices, ring_sum(): running = lax.ppermute(running, axis, pairs)  120 us
    pallas_call x8, Pallas kernels, correlate(): pl.pallas_call(correlate_kernel, grid_spec=pltpu.PrefetchScalarGridSpec(n...  86.8 us
    ppermute x4, waiting for transfers between devices, per_device(): running = add(lax.ppermute(running, 'tm', y_pairs), vis[step, chunk])  70.6 us
    psum x1, blocking collectives, per_device(): stats = lax.psum(stats, ('chan', 'tm')) / CHANNELS  37.9 us
    pallas_call x1, Pallas kernels, transform(): pl.pallas_call(lambda p, f, c, o, t: transform_kernel(p, f, c, o, t), gri...  34.2 us
    ppermute x18, starting transfers between devices, ring_sum(): running = lax.ppermute(running, axis, pairs)  20.5 us
    unnamed x54, local copies, waits for them, and re-layouts  19.5 us
    convert_element_type x21, other arithmetic, add(): return (left.astype(F32) + right.astype(F32)).astype(BF16)  13.9 us
  transfers between devices with their start and end apart: 22, of which 18 were waited for; matrix products, arithmetic and copies ran while one was open for 4% of the time, Pallas kernels for 0%

profile of v1, /device:TPU:0, one launch (start us, length us, event | category | flops | bytes accessed | tf_op | source)
XLA Modules:
  0.0 437.1 jit_solution(8029813142570693126)
XLA Ops:
  1.5 11.2 %correlate.11 = (bf16[6,256,512]{2,1,0:T(8,128)(2,1)}, bf16[4,256,256]{2,1,0:T(8,128)(2,1)S(1)}) custom-call(s32[3]{0:T(128)S(1)} %get-tuple-element.45.scalars, bf16[8,2048,2,512]{3,2,1,0:T(2,128)(2,1)} %x_ref.15), custom_call_target="tpu_custom_call" | custom-call | flops 1073741824 | bytes 8388608 | tf_op jit(solution)/shard_map/correlate/pallas_call | solution.py:87
  12.7 10.5 %correlate.15 = (bf16[6,256,512]{2,1,0:T(8,128)(2,1)S(1)}, bf16[4,256,256]{2,1,0:T(8,128)(2,1)S(1)}) custom-call(s32[3]{0:T(128)S(1)} %get-tuple-element.42.scalars, bf16[8,2048,2,512]{3,2,1,0:T(2,128)(2,1)} %x_ref.15), custom_call_target="tpu_custom_call" | custom-call | flops 1073741824 | bytes 8388608 | tf_op jit(solution)/shard_map/correlate/pallas_call | solution.py:87
  24.0 11.2 %correlate.10 = (bf16[6,256,512]{2,1,0:T(8,128)(2,1)}, bf16[4,256,256]{2,1,0:T(8,128)(2,1)S(1)}) custom-call(s32[3]{0:T(128)S(1)} %get-tuple-element.44.scalars, bf16[8,2048,2,512]{3,2,1,0:T(2,128)(2,1)} %x_ref.15), custom_call_target="tpu_custom_call" | custom-call | flops 1073741824 | bytes 8388608 | tf_op jit(solution)/shard_map/correlate/pallas_call | solution.py:87
  36.1 10.5 %correlate.14 = (bf16[6,256,512]{2,1,0:T(8,128)(2,1)S(1)}, bf16[4,256,256]{2,1,0:T(8,128)(2,1)S(1)}) custom-call(s32[3]{0:T(128)S(1)} %get-tuple-element.46.scalars, bf16[8,2048,2,512]{3,2,1,0:T(2,128)(2,1)} %x_ref.15), custom_call_target="tpu_custom_call" | custom-call | flops 1073741824 | bytes 8388608 | tf_op jit(solution)/shard_map/correlate/pallas_call | solution.py:87
  48.6 11.2 %correlate.9 = (bf16[6,256,512]{2,1,0:T(8,128)(2,1)}, bf16[4,256,256]{2,1,0:T(8,128)(2,1)S(1)}) custom-call(s32[3]{0:T(128)S(1)} %get-tuple-element.43.scalars, bf16[8,2048,2,512]{3,2,1,0:T(2,128)(2,1)} %x_ref.15), custom_call_target="tpu_custom_call" | custom-call | flops 1073741824 | bytes 8388608 | tf_op jit(solution)/shard_map/correlate/pallas_call | solution.py:87
  60.5 10.5 %correlate.13 = (bf16[6,256,512]{2,1,0:T(8,128)(2,1)S(1)}, bf16[4,256,256]{2,1,0:T(8,128)(2,1)S(1)}) custom-call(s32[3]{0:T(128)S(1)} %get-tuple-element.48.scalars, bf16[8,2048,2,512]{3,2,1,0:T(2,128)(2,1)} %x_ref.15), custom_call_target="tpu_custom_call" | custom-call | flops 1073741824 | bytes 8388608 | tf_op jit(solution)/shard_map/correlate/pallas_call | solution.py:87
  73.0 11.2 %correlate.8 = (bf16[6,256,512]{2,1,0:T(8,128)(2,1)}, bf16[4,256,256]{2,1,0:T(8,128)(2,1)S(1)}) custom-call(s32[3]{0:T(128)S(1)} %get-tuple-element.49.scalars, bf16[8,2048,2,512]{3,2,1,0:T(2,128)(2,1)} %x_ref.15), custom_call_target="tpu_custom_call" | custom-call | flops 1073741824 | bytes 8388608 | tf_op jit(solution)/shard_map/correlate/pallas_call | solution.py:87
  84.2 10.5 %correlate.12 = (bf16[6,256,512]{2,1,0:T(8,128)(2,1)S(1)}, bf16[4,256,256]{2,1,0:T(8,128)(2,1)S(1)}) custom-call(s32[3]{0:T(128)S(1)} %get-tuple-element.47.scalars, bf16[8,2048,2,512]{3,2,1,0:T(2,128)(2,1)} %x_ref.15), custom_call_target="tpu_custom_call" | custom-call | flops 1073741824 | bytes 8388608 | tf_op jit(solution)/shard_map/correlate/pallas_call | solution.py:87
  96.5 5.5 %multiply_cosine_fusion = (f32[1,2048,128]{2,1,0:T(8,128)}, f32[1,2048,128]{2,1,0:T(8,128)}) fusion(f32[128]{0:T(128)S(1)} %convert_multiply_fusion.1, f32[2048]{0:T(1024)S(1)} %add_multiply_fusion), kind=kLoop, calls=%fused_computation.9 | loop fusion | flops 262144 | bytes 2105856 | tf_op jit(solution)/shard_map/cos | solution.py:168
  115.3 34.2 %transform.1 = f32[256,2,2,1024]{3,2,1,0:T(2,128)S(1)} custom-call(bf16[4,2048,256]{2,1,0:T(8,128)(2,1)S(1)} %copy-done.17, f32[2,2048,128]{2,1,0:T(8,128)S(1)} %pad_maximum_fusion.f, f32[2048,16]{1,0:T(8,128)S(1)} %bitcast.117), custom_call_target="tpu_custom_call" | custom-call | flops 8589934592 | bytes 16777216 | tf_op jit(solution)/shard_map/transform/pallas_call | solution.py:141
  149.4 3.3 convert_element_type.290
  152.8 4.6 %constant_dynamic-slice_fusion.1 = (bf16[4,2,2,1,8,2,2,1024]{7,6,5,4,3,2,1,0:T(2,128)(2,1)}, bf16[4,2,2,1,8,2,2,1024]{7,6,5,4,3,2,1,0:T(2,128)(2,1)S(1)}) fusion(bf16[4,2,2,2,8,2,2,1024]{7,6,5,4,3,2,1,0:T(2,128)(2,1)} %bitcast.118, s32[]{:T(128)S(6)} %select_n.72, s32[]{:T(128)S(6)} %select_n.71), kind=kLoop, calls=%fused_computation.70 | loop fusion | bytes 4194312 | tf_op jit(solution)/shard_map/jit(dynamic_index_in_dim)/dynamic_slice | solution.py:337
  162.4 2.7 fusion
  167.2 2.9 collective-permute-start.1
  172.5 10.2 %collective-permute-done.1 = bf16[4,2,8,2,2,1024]{5,4,3,2,0,1:T(2,128)(2,1)} collective-permute-done((bf16[4,2,8,2,2,1024]{5,4,3,2,0,1:T(2,128)(2,1)}, bf16[4,2,8,2,2,1024]{5,4,3,2,0,1:T(2,128)(2,1)}, u32[]{:S(2)}, u32[]{:S(2)}) %collective-permute-start.1) | collective-permute-done | bytes 524320 | tf_op jit(solution)/shard_map/ppermute | solution.py:268
  186.4 11.4 %collective-permute-done.18 = bf16[6,256,512]{2,1,0:T(8,128)(2,1)} collective-permute-done((bf16[6,256,512]{2,1,0:T(8,128)(2,1)}, bf16[6,256,512]{2,1,0:T(8,128)(2,1)}, u32[]{:S(2)}, u32[]{:S(2)}) %collective-permute-start.18) | collective-permute-done | bytes 1572896 | tf_op jit(solution)/shard_map/ppermute | solution.py:308
  201.9 29.6 %collective-permute-done.14 = bf16[6,256,512]{2,1,0:T(8,128)(2,1)} collective-permute-done((bf16[6,256,512]{2,1,0:T(8,128)(2,1)}, bf16[6,256,512]{2,1,0:T(8,128)(2,1)}, u32[]{:S(2)}, u32[]{:S(2)}) %collective-permute-start.14) | collective-permute-done | bytes 1572896 | tf_op jit(solution)/shard_map/ppermute | solution.py:308
  235.7 29.6 %collective-permute-done.10 = bf16[6,256,512]{2,1,0:T(8,128)(2,1)} collective-permute-done((bf16[6,256,512]{2,1,0:T(8,128)(2,1)}, bf16[6,256,512]{2,1,0:T(8,128)(2,1)}, u32[]{:S(2)}, u32[]{:S(2)}) %collective-permute-start.10) | collective-permute-done | bytes 1572896 | tf_op jit(solution)/shard_map/ppermute | solution.py:308
  269.3 35.0 %collective-permute-done.2 = bf16[4,8,2,2,1024]{4,3,2,1,0:T(2,128)(2,1)S(1)} collective-permute-done((bf16[4,8,2,2,1024]{4,3,2,1,0:T(2,128)(2,1)S(1)}, bf16[4,8,2,2,1024]{4,3,2,1,0:T(2,128)(2,1)S(1)}, u32[]{:S(2)}, u32[]{:S(2)}) %collective-permute-start.2) | collective-permute-done | bytes 262176 | tf_op jit(solution)/shard_map/ppermute | solution.py:268
  312.5 5.2 %collective-permute-done.4 = bf16[8,2,2,1024]{3,2,1,0:T(2,128)(2,1)S(1)} collective-permute-done((bf16[8,2,2,1024]{3,2,1,0:T(2,128)(2,1)S(1)}, bf16[8,2,2,1024]{3,2,1,0:T(2,128)(2,1)S(1)}, u32[]{:S(2)}, u32[]{:S(2)}) %collective-permute-start.4) | collective-permute-done | bytes 65568 | tf_op jit(solution)/shard_map/ppermute | solution.py:268
  319.5 3.8 collective-permute-start.12
  323.3 2.8 collective-permute-done.7
  328.3 7.7 %collective-permute-done.20 = bf16[6,64,512]{2,1,0:T(8,128)(2,1)S(1)} collective-permute-done((bf16[6,64,512]{2,1,0:T(8,128)(2,1)S(1)}, bf16[6,64,512]{2,1,0:T(8,128)(2,1)S(1)}, u32[]{:S(2)}, u32[]{:S(2)}) %collective-permute-start.20) | collective-permute-done | bytes 393248 | tf_op jit(solution)/shard_map/ppermute | solution.py:268
  336.2 8.2 %collective-permute-done.16 = bf16[6,64,512]{2,1,0:T(8,128)(2,1)S(1)} collective-permute-done((bf16[6,64,512]{2,1,0:T(8,128)(2,1)S(1)}, bf16[6,64,512]{2,1,0:T(8,128)(2,1)S(1)}, u32[]{:S(2)}, u32[]{:S(2)}) %collective-permute-start.16) | collective-permute-done | bytes 393248 | tf_op jit(solution)/shard_map/ppermute | solution.py:268
  344.6 8.2 %collective-permute-done.12 = bf16[6,64,512]{2,1,0:T(8,128)(2,1)S(1)} collective-permute-done((bf16[6,64,512]{2,1,0:T(8,128)(2,1)S(1)}, bf16[6,64,512]{2,1,0:T(8,128)(2,1)S(1)}, u32[]{:S(2)}, u32[]{:S(2)}) %collective-permute-start.12) | collective-permute-done | bytes 393248 | tf_op jit(solution)/shard_map/ppermute | solution.py:268
  353.0 8.2 %collective-permute-done.8 = bf16[6,64,512]{2,1,0:T(8,128)(2,1)S(1)} collective-permute-done((bf16[6,64,512]{2,1,0:T(8,128)(2,1)S(1)}, bf16[6,64,512]{2,1,0:T(8,128)(2,1)S(1)}, u32[]{:S(2)}, u32[]{:S(2)}) %collective-permute-start.8) | collective-permute-done | bytes 393248 | tf_op jit(solution)/shard_map/ppermute | solution.py:268
  361.4 8.2 %collective-permute-done.21 = bf16[6,64,512]{2,1,0:T(8,128)(2,1)S(1)} collective-permute-done((bf16[6,64,512]{2,1,0:T(8,128)(2,1)S(1)}, bf16[6,64,512]{2,1,0:T(8,128)(2,1)S(1)}, u32[]{:S(2)}, u32[]{:S(2)}) %collective-permute-start.21) | collective-permute-done | bytes 393248 | tf_op jit(solution)/shard_map/ppermute | solution.py:268
  369.8 8.3 %collective-permute-done.17 = bf16[6,64,512]{2,1,0:T(8,128)(2,1)S(1)} collective-permute-done((bf16[6,64,512]{2,1,0:T(8,128)(2,1)S(1)}, bf16[6,64,512]{2,1,0:T(8,128)(2,1)S(1)}, u32[]{:S(2)}, u32[]{:S(2)}) %collective-permute-start.17) | collective-permute-done | bytes 393248 | tf_op jit(solution)/shard_map/ppermute | solution.py:268
  378.2 8.3 %collective-permute-done.13 = bf16[6,64,512]{2,1,0:T(8,128)(2,1)S(1)} collective-permute-done((bf16[6,64,512]{2,1,0:T(8,128)(2,1)S(1)}, bf16[6,64,512]{2,1,0:T(8,128)(2,1)S(1)}, u32[]{:S(2)}, u32[]{:S(2)}) %collective-permute-start.13) | collective-permute-done | bytes 393248 | tf_op jit(solution)/shard_map/ppermute | solution.py:268
  386.6 6.1 %collective-permute-done.9 = bf16[6,64,512]{2,1,0:T(8,128)(2,1)S(1)} collective-permute-done((bf16[6,64,512]{2,1,0:T(8,128)(2,1)S(1)}, bf16[6,64,512]{2,1,0:T(8,128)(2,1)S(1)}, u32[]{:S(2)}, u32[]{:S(2)}) %collective-permute-start.9) | collective-permute-done | bytes 393248 | tf_op jit(solution)/shard_map/ppermute | solution.py:268
  393.1 3.6 statistics.1
  396.9 37.9 %psum.7 = f32[16,256]{1,0:T(8,128)S(1)} all-reduce(f32[16,256]{1,0:T(8,128)S(1)} %bitcast.136), channel_id=1, replica_groups=mesh['chan'=4,'tm'=8] {'chan','tm'}, use_global_device_ids=true, to_apply=%region_0.1 | all-reduce | flops 4096 | bytes 32768 | tf_op jit(solution)/shard_map/psum | solution.py:344
  (142 shorter events, 63.2 us)
Async XLA Ops:
  12.7 10.5 %copy-start.7 = (bf16[4,256,256]{2,1,0:T(8,128)(2,1)}, bf16[4,256,256]{2,1,0:T(8,128)(2,1)S(1)}, u32[]{:S(2)}) copy-start(bf16[4,256,256]{2,1,0:T(8,128)(2,1)S(1)} %get-tuple-element.21) | copy-start | bytes 1572868
  24.0 12.0 %copy-start.22 = (s32[2]{0:T(128)S(1)}, s32[2]{0:T(128)}, u32[]{:S(2)}) copy-start(s32[2]{0:T(128)} %stations_ref.1) | copy-start | bytes 28
  84.2 11.3 %copy-start.21 = (s32[8192]{0:T(1024)S(1)}, s32[8192]{0:T(1024)}, u32[]{:S(2)}) copy-start(s32[8192]{0:T(1024)} %param.5) | copy-start | bytes 98308
  103.8 3.9 copy-start.8
  103.8 4.8 %copy-start.16 = (bf16[4,256,256]{2,1,0:T(8,128)(2,1)S(1)}, bf16[4,256,256]{2,1,0:T(8,128)(2,1)}, u32[]{:S(2)}) copy-start(bf16[4,256,256]{2,1,0:T(8,128)(2,1)} %copy-done.15) | copy-start | bytes 1572868
  103.8 5.6 %copy-start.13 = (bf16[4,256,256]{2,1,0:T(8,128)(2,1)S(1)}, bf16[4,256,256]{2,1,0:T(8,128)(2,1)}, u32[]{:S(2)}) copy-start(bf16[4,256,256]{2,1,0:T(8,128)(2,1)} %copy-done.12) | copy-start | bytes 1572868
  105.8 4.4 %copy-start.11 = (bf16[4,256,256]{2,1,0:T(8,128)(2,1)S(1)}, bf16[4,256,256]{2,1,0:T(8,128)(2,1)}, u32[]{:S(2)}) copy-start(bf16[4,256,256]{2,1,0:T(8,128)(2,1)} %copy-done.10) | copy-start | bytes 1572868
  107.7 3.3 copy-start.6
  159.3 3.1 collective-permute-start
  159.8 38.1 %collective-permute-start.18 = (bf16[6,256,512]{2,1,0:T(8,128)(2,1)}, bf16[6,256,512]{2,1,0:T(8,128)(2,1)}, u32[]{:S(2)}, u32[]{:S(2)}) collective-permute-start(bf16[6,256,512]{2,1,0:T(8,128)(2,1)} %get-tuple-element.32), channel_id=1, source_target_pairs={{0,1},{1,0},{2,3},{3,2},{4,5},{5,4},{6,7},{7,6},{8,9},{9,8},{10,11... | collective-permute-start | bytes 4718600 | tf_op jit(solution)/shard_map/ppermute | solution.py:308
  162.3 69.3 %collective-permute-start.14 = (bf16[6,256,512]{2,1,0:T(8,128)(2,1)}, bf16[6,256,512]{2,1,0:T(8,128)(2,1)}, u32[]{:S(2)}, u32[]{:S(2)}) collective-permute-start(bf16[6,256,512]{2,1,0:T(8,128)(2,1)} %get-tuple-element.30), channel_id=1, source_target_pairs={{0,1},{1,0},{2,3},{3,2},{4,5},{5,4},{6,7},{7,6},{8,9},{9,8},{10,11... | collective-permute-start | bytes 4718600 | tf_op jit(solution)/shard_map/ppermute | solution.py:308
  167.2 15.4 %collective-permute-start.1 = (bf16[4,2,8,2,2,1024]{5,4,3,2,0,1:T(2,128)(2,1)}, bf16[4,2,8,2,2,1024]{5,4,3,2,0,1:T(2,128)(2,1)}, u32[]{:S(2)}, u32[]{:S(2)}) collective-permute-start(bf16[4,2,8,2,2,1024]{5,4,3,2,0,1:T(2,128)(2,1)} %dynamic-slice_bitcast_fusion), channel_id=1, source_target_pairs={{0,16},{8,24},{16,0},{24,8},{1,17},{9,25},{17,1},{25,9},{2,18},{10... | collective-permute-start | bytes 1572872 | tf_op jit(solution)/shard_map/ppermute | solution.py:268
  170.1 95.1 %collective-permute-start.10 = (bf16[6,256,512]{2,1,0:T(8,128)(2,1)}, bf16[6,256,512]{2,1,0:T(8,128)(2,1)}, u32[]{:S(2)}, u32[]{:S(2)}) collective-permute-start(bf16[6,256,512]{2,1,0:T(8,128)(2,1)} %get-tuple-element.28), channel_id=1, source_target_pairs={{0,1},{1,0},{2,3},{3,2},{4,5},{5,4},{6,7},{7,6},{8,9},{9,8},{10,11... | collective-permute-start | bytes 4718600 | tf_op jit(solution)/shard_map/ppermute | solution.py:308
  171.6 134.9 %collective-permute-start.6 = (bf16[6,256,512]{2,1,0:T(8,128)(2,1)}, bf16[6,256,512]{2,1,0:T(8,128)(2,1)}, u32[]{:S(2)}, u32[]{:S(2)}) collective-permute-start(bf16[6,256,512]{2,1,0:T(8,128)(2,1)} %get-tuple-element.26), channel_id=1, source_target_pairs={{0,1},{1,0},{2,3},{3,2},{4,5},{5,4},{6,7},{7,6},{8,9},{9,8},{10,11... | collective-permute-start | bytes 4718600 | tf_op jit(solution)/shard_map/ppermute | solution.py:308
  184.6 119.7 %collective-permute-start.2 = (bf16[4,8,2,2,1024]{4,3,2,1,0:T(2,128)(2,1)S(1)}, bf16[4,8,2,2,1024]{4,3,2,1,0:T(2,128)(2,1)S(1)}, u32[]{:S(2)}, u32[]{:S(2)}) collective-permute-start(bf16[4,8,2,2,1024]{4,3,2,1,0:T(2,128)(2,1)S(1)} %dynamic-slice_bitcast_fusion.5), channel_id=1, source_target_pairs={{0,1},{1,0},{2,3},{3,2},{4,5},{5,4},{6,7},{7,6},{8,9},{9,8},{10,11... | collective-permute-start | bytes 786440 | tf_op jit(solution)/shard_map/ppermute | solution.py:268
  197.8 33.7 %copy-start.3 = (bf16[6,256,512]{2,1,0:T(8,128)(2,1)S(1)}, bf16[6,256,512]{2,1,0:T(8,128)(2,1)}, u32[]{:S(2)}) copy-start(bf16[6,256,512]{2,1,0:T(8,128)(2,1)} %copy-done.2) | copy-start | bytes 4718596
  199.8 118.0 %collective-permute-start.19 = (bf16[6,64,512]{2,1,0:T(8,128)(2,1)S(1)}, bf16[6,64,512]{2,1,0:T(8,128)(2,1)S(1)}, u32[]{:S(2)}, u32[]{:S(2)}) collective-permute-start(bf16[6,64,512]{2,1,0:T(8,128)(2,1)S(1)} %dynamic-slice_bitcast_fusion.1), channel_id=1, source_target_pairs={{0,2},{1,3},{2,4},{3,5},{4,6},{5,7},{6,0},{7,1},{8,10},{9,11},{10,... | collective-permute-start | bytes 1179656 | tf_op jit(solution)/shard_map/ppermute | solution.py:268
  231.5 33.7 %copy-start.1 = (bf16[6,256,512]{2,1,0:T(8,128)(2,1)S(1)}, bf16[6,256,512]{2,1,0:T(8,128)(2,1)}, u32[]{:S(2)}) copy-start(bf16[6,256,512]{2,1,0:T(8,128)(2,1)} %copy-done) | copy-start | bytes 4718596
  233.6 84.4 %collective-permute-start.15 = (bf16[6,64,512]{2,1,0:T(8,128)(2,1)S(1)}, bf16[6,64,512]{2,1,0:T(8,128)(2,1)S(1)}, u32[]{:S(2)}, u32[]{:S(2)}) collective-permute-start(bf16[6,64,512]{2,1,0:T(8,128)(2,1)S(1)} %dynamic-slice_bitcast_fusion.2), channel_id=1, source_target_pairs={{0,2},{1,3},{2,4},{3,5},{4,6},{5,7},{6,0},{7,1},{8,10},{9,11},{10,... | collective-permute-start | bytes 1179656 | tf_op jit(solution)/shard_map/ppermute | solution.py:268
  267.2 52.2 %collective-permute-start.11 = (bf16[6,64,512]{2,1,0:T(8,128)(2,1)S(1)}, bf16[6,64,512]{2,1,0:T(8,128)(2,1)S(1)}, u32[]{:S(2)}, u32[]{:S(2)}) collective-permute-start(bf16[6,64,512]{2,1,0:T(8,128)(2,1)S(1)} %dynamic-slice_bitcast_fusion.3), channel_id=1, source_target_pairs={{0,2},{1,3},{2,4},{3,5},{4,6},{5,7},{6,0},{7,1},{8,10},{9,11},{10,... | collective-permute-start | bytes 1179656 | tf_op jit(solution)/shard_map/ppermute | solution.py:268
  304.6 6.1 %collective-permute-start.3 = (bf16[8,2,2,1024]{3,2,1,0:T(2,128)(2,1)S(1)}, bf16[8,2,2,1024]{3,2,1,0:T(2,128)(2,1)S(1)}, u32[]{:S(2)}, u32[]{:S(2)}) collective-permute-start(bf16[8,2,2,1024]{3,2,1,0:T(2,128)(2,1)S(1)} %dynamic-slice_bitcast_fusion.6), channel_id=1, source_target_pairs={{0,2},{1,3},{2,4},{3,5},{4,6},{5,7},{6,0},{7,1},{8,10},{9,11},{10,... | collective-permute-start | bytes 196616 | tf_op jit(solution)/shard_map/ppermute | solution.py:268
  310.8 6.9 %collective-permute-start.4 = (bf16[8,2,2,1024]{3,2,1,0:T(2,128)(2,1)S(1)}, bf16[8,2,2,1024]{3,2,1,0:T(2,128)(2,1)S(1)}, u32[]{:S(2)}, u32[]{:S(2)}) collective-permute-start(bf16[8,2,2,1024]{3,2,1,0:T(2,128)(2,1)S(1)} %fusion.17), channel_id=1, source_target_pairs={{0,2},{1,3},{2,4},{3,5},{4,6},{5,7},{6,0},{7,1},{8,10},{9,11},{10,... | collective-permute-start | bytes 196616 | tf_op jit(solution)/shard_map/ppermute | solution.py:268
  310.9 15.2 %collective-permute-start.7 = (bf16[6,64,512]{2,1,0:T(8,128)(2,1)S(1)}, bf16[6,64,512]{2,1,0:T(8,128)(2,1)S(1)}, u32[]{:S(2)}, u32[]{:S(2)}) collective-permute-start(bf16[6,64,512]{2,1,0:T(8,128)(2,1)S(1)} %dynamic-slice_bitcast_fusion.4), channel_id=1, source_target_pairs={{0,2},{1,3},{2,4},{3,5},{4,6},{5,7},{6,0},{7,1},{8,10},{9,11},{10,... | collective-permute-start | bytes 1179656 | tf_op jit(solution)/shard_map/ppermute | solution.py:268
  317.8 9.8 %collective-permute-start.5 = (bf16[8,2,2,1024]{3,2,1,0:T(2,128)(2,1)S(1)}, bf16[8,2,2,1024]{3,2,1,0:T(2,128)(2,1)S(1)}, u32[]{:S(2)}, u32[]{:S(2)}) collective-permute-start(bf16[8,2,2,1024]{3,2,1,0:T(2,128)(2,1)S(1)} %fusion.16), channel_id=1, source_target_pairs={{0,2},{1,3},{2,4},{3,5},{4,6},{5,7},{6,0},{7,1},{8,10},{9,11},{10,... | collective-permute-start | bytes 196616 | tf_op jit(solution)/shard_map/ppermute | solution.py:268
  318.0 18.0 %collective-permute-start.20 = (bf16[6,64,512]{2,1,0:T(8,128)(2,1)S(1)}, bf16[6,64,512]{2,1,0:T(8,128)(2,1)S(1)}, u32[]{:S(2)}, u32[]{:S(2)}) collective-permute-start(bf16[6,64,512]{2,1,0:T(8,128)(2,1)S(1)} %fusion.4), channel_id=1, source_target_pairs={{0,2},{1,3},{2,4},{3,5},{4,6},{5,7},{6,0},{7,1},{8,10},{9,11},{10,... | collective-permute-start | bytes 1179656 | tf_op jit(solution)/shard_map/ppermute | solution.py:268
  318.2 26.2 %collective-permute-start.16 = (bf16[6,64,512]{2,1,0:T(8,128)(2,1)S(1)}, bf16[6,64,512]{2,1,0:T(8,128)(2,1)S(1)}, u32[]{:S(2)}, u32[]{:S(2)}) collective-permute-start(bf16[6,64,512]{2,1,0:T(8,128)(2,1)S(1)} %fusion.7), channel_id=1, source_target_pairs={{0,2},{1,3},{2,4},{3,5},{4,6},{5,7},{6,0},{7,1},{8,10},{9,11},{10,... | collective-permute-start | bytes 1179656 | tf_op jit(solution)/shard_map/ppermute | solution.py:268
  319.5 33.3 %collective-permute-start.12 = (bf16[6,64,512]{2,1,0:T(8,128)(2,1)S(1)}, bf16[6,64,512]{2,1,0:T(8,128)(2,1)S(1)}, u32[]{:S(2)}, u32[]{:S(2)}) collective-permute-start(bf16[6,64,512]{2,1,0:T(8,128)(2,1)S(1)} %fusion.10), channel_id=1, source_target_pairs={{0,2},{1,3},{2,4},{3,5},{4,6},{5,7},{6,0},{7,1},{8,10},{9,11},{10,... | collective-permute-start | bytes 1179656 | tf_op jit(solution)/shard_map/ppermute | solution.py:268
  326.3 35.0 %collective-permute-start.8 = (bf16[6,64,512]{2,1,0:T(8,128)(2,1)S(1)}, bf16[6,64,512]{2,1,0:T(8,128)(2,1)S(1)}, u32[]{:S(2)}, u32[]{:S(2)}) collective-permute-start(bf16[6,64,512]{2,1,0:T(8,128)(2,1)S(1)} %fusion.13), channel_id=1, source_target_pairs={{0,2},{1,3},{2,4},{3,5},{4,6},{5,7},{6,0},{7,1},{8,10},{9,11},{10,... | collective-permute-start | bytes 1179656 | tf_op jit(solution)/shard_map/ppermute | solution.py:268
  336.1 33.6 %collective-permute-start.21 = (bf16[6,64,512]{2,1,0:T(8,128)(2,1)S(1)}, bf16[6,64,512]{2,1,0:T(8,128)(2,1)S(1)}, u32[]{:S(2)}, u32[]{:S(2)}) collective-permute-start(bf16[6,64,512]{2,1,0:T(8,128)(2,1)S(1)} %fusion.3), channel_id=1, source_target_pairs={{0,2},{1,3},{2,4},{3,5},{4,6},{5,7},{6,0},{7,1},{8,10},{9,11},{10,... | collective-permute-start | bytes 1179656 | tf_op jit(solution)/shard_map/ppermute | solution.py:268
  344.5 33.6 %collective-permute-start.17 = (bf16[6,64,512]{2,1,0:T(8,128)(2,1)S(1)}, bf16[6,64,512]{2,1,0:T(8,128)(2,1)S(1)}, u32[]{:S(2)}, u32[]{:S(2)}) collective-permute-start(bf16[6,64,512]{2,1,0:T(8,128)(2,1)S(1)} %fusion.6), channel_id=1, source_target_pairs={{0,2},{1,3},{2,4},{3,5},{4,6},{5,7},{6,0},{7,1},{8,10},{9,11},{10,... | collective-permute-start | bytes 1179656 | tf_op jit(solution)/shard_map/ppermute | solution.py:268
  352.9 33.6 %collective-permute-start.13 = (bf16[6,64,512]{2,1,0:T(8,128)(2,1)S(1)}, bf16[6,64,512]{2,1,0:T(8,128)(2,1)S(1)}, u32[]{:S(2)}, u32[]{:S(2)}) collective-permute-start(bf16[6,64,512]{2,1,0:T(8,128)(2,1)S(1)} %fusion.9), channel_id=1, source_target_pairs={{0,2},{1,3},{2,4},{3,5},{4,6},{5,7},{6,0},{7,1},{8,10},{9,11},{10,... | collective-permute-start | bytes 1179656 | tf_op jit(solution)/shard_map/ppermute | solution.py:268
  361.4 31.4 %collective-permute-start.9 = (bf16[6,64,512]{2,1,0:T(8,128)(2,1)S(1)}, bf16[6,64,512]{2,1,0:T(8,128)(2,1)S(1)}, u32[]{:S(2)}, u32[]{:S(2)}) collective-permute-start(bf16[6,64,512]{2,1,0:T(8,128)(2,1)S(1)} %fusion.12), channel_id=1, source_target_pairs={{0,2},{1,3},{2,4},{3,5},{4,6},{5,7},{6,0},{7,1},{8,10},{9,11},{10,... | collective-permute-start | bytes 1179656 | tf_op jit(solution)/shard_map/ppermute | solution.py:268
  (13 other events, 18.1 us)

commit v2 on v1

--- a/solution.py
+++ b/solution.py
@@ -19,35 +19,42 @@
 BF16 = jnp.bfloat16
 
 
-def correlate_kernel(scalars, x_ref, vis_ref, pol_ref):
+def selectors(window_stations, times, parts, inputs):
+    depth, columns = times * GROUP * parts, 8 * GROUP
+    row = jnp.arange(depth, dtype=jnp.int32)[:, None]
+    col = jnp.arange(columns, dtype=jnp.int32)[None, :]
+    same = (row // parts) % GROUP == col % GROUP
+    real_row, real_col = row % parts == 0, col < 4 * GROUP
+    masks = jnp.stack(
+        [
+            (same & real_col).astype(F32),
+            (same & ~real_col & real_row).astype(F32),
+            -(same & ~real_col & ~real_row).astype(F32),
+        ],
+        0,
+    )
+    feeds = (2 * window_stations[:, None] + jnp.arange(2, dtype=jnp.int32)[None, :]).reshape(-1)
+    lane = jnp.arange(inputs, dtype=jnp.int32)[:, None]
+    pick = (lane == jnp.tile(jnp.repeat(feeds, GROUP), 2)[None, :]).astype(BF16)
+    pair_sum = (lane // 2 == jnp.arange(inputs // 2, dtype=jnp.int32)[None, :]).astype(BF16)
+    return masks, pick, pair_sum
+
+
+def correlate_kernel(scalars, x_ref, mask_ref, pick_ref, pair_ref, vis_ref, pol_ref):
     times, _, parts, inputs = x_ref.shape
     depth = times * GROUP * parts
-    columns = 8 * GROUP
-    row = lax.broadcasted_iota(jnp.int32, (depth, columns), 0)
-    col = lax.broadcasted_iota(jnp.int32, (depth, columns), 1)
-    same_channel = lax.rem(lax.div(row, parts), GROUP) == lax.rem(col, GROUP)
-    is_real_row = lax.rem(row, parts) == 0
-    is_real_col = col < 4 * GROUP
-    feed = lax.rem(lax.div(lax.broadcasted_iota(jnp.int32, (inputs, columns), 1), GROUP), 4)
-    station = jnp.where(feed < 2, scalars[1], scalars[2])
-    pick = (
-        lax.broadcasted_iota(jnp.int32, (inputs, columns), 0) == 2 * station + lax.rem(feed, 2)
-    ).astype(F32).astype(BF16)
-    first_feed = lax.rem(lax.broadcasted_iota(jnp.int32, (GROUP, inputs), 1), 2) == 0
-    pair_sum = (
-        lax.div(lax.broadcasted_iota(jnp.int32, (inputs, inputs // 2), 0), 2)
-        == lax.broadcasted_iota(jnp.int32, (inputs, inputs // 2), 1)
-    ).astype(F32).astype(BF16)
+    first_feed = (lax.broadcasted_iota(jnp.int32, (GROUP, inputs), 1) & 1) == 0
 
     def body(step, carry):
         start = pl.multiple_of(step * GROUP, GROUP)
         here = pl.ds(start, GROUP)
         x = x_ref[:, here, :, :].reshape(depth, inputs)
-        picked = jnp.dot(x, pick, preferred_element_type=F32)
-        swapped = jnp.where(
-            is_real_row, pltpu.roll(picked, depth - 1, 0), -pltpu.roll(picked, 1, 0)
-        )
-        left = jnp.where(same_channel, jnp.where(is_real_col, picked, swapped), 0.0).astype(BF16)
+        picked = jnp.dot(x, pick_ref[...], preferred_element_type=F32)
+        left = (
+            picked * mask_ref[0]
+            + pltpu.roll(picked, depth - 1, 0) * mask_ref[1]
+            + pltpu.roll(picked, 1, 0) * mask_ref[2]
+        ).astype(BF16)
         out = lax.dot_general(
             left, x, (((0,), (0,)), ((), ())), preferred_element_type=F32
         )
@@ -70,7 +77,7 @@
             pols.append(jnp.where(first_feed, x_real - y_imag, -(y_real + x_imag)))
             pols.append(jnp.where(first_feed, x_imag + y_real, x_real - y_imag))
         pol = jnp.concatenate([(0.5 * value).astype(BF16) for value in pols], 0)
-        summed = jnp.dot(pol, pair_sum, preferred_element_type=F32).astype(BF16)
+        summed = jnp.dot(pol, pair_ref[...], preferred_element_type=F32).astype(BF16)
         for index in range(4):
             pol_ref[index, here, :] = summed[index * GROUP : (index + 1) * GROUP]
         return carry
@@ -78,18 +85,21 @@
     lax.fori_loop(0, x_ref.shape[1] // GROUP, body, 0, unroll=2)
 
 
-def correlate(voltages, window_stations, first, count):
+def correlate(voltages, chosen, first, count):
     times, _, parts, inputs = voltages.shape
     block = math.gcd(count, 64)
-    scalars = jnp.concatenate(
-        [jnp.reshape(lax.div(first, block), (1,)), window_stations]
-    ).astype(jnp.int32)
+    scalars = jnp.reshape(lax.div(first, block), (1,)).astype(jnp.int32)
     return pl.pallas_call(
         correlate_kernel,
         grid_spec=pltpu.PrefetchScalarGridSpec(
             num_scalar_prefetch=1,
             grid=(count // block,),
-            in_specs=[pl.BlockSpec((times, block, parts, inputs), lambda i, s: (0, s[0] + i, 0, 0))],
+            in_specs=[
+                pl.BlockSpec((times, block, parts, inputs), lambda i, s: (0, s[0] + i, 0, 0)),
+                pl.BlockSpec(chosen[0].shape, lambda i, s: (0, 0, 0)),
+                pl.BlockSpec(chosen[1].shape, lambda i, s: (0, 0)),
+                pl.BlockSpec(chosen[2].shape, lambda i, s: (0, 0)),
+            ],
             out_specs=[
                 pl.BlockSpec((6, block, inputs), lambda i, s: (0, i, 0)),
                 pl.BlockSpec((4, block, inputs // 2), lambda i, s: (0, i, 0)),
@@ -104,13 +114,13 @@
             flops=count * 16 * 2 * 512 * 256, bytes_accessed=count * 16 * 1024 * 2, transcendentals=0
         ),
         name="correlate",
-    )(scalars, voltages)
-
-
-def transform_kernel(pol_ref, fine_ref, coarse_ref, out_ref, table):
+    )(scalars, voltages, *chosen)
+
+
+def transform_kernel(pol_ref, fine_ref, coarse_ref, out_ref, table, total):
     @pl.when(pl.program_id(0) == 0)
     def _():
-        out_ref[...] = jnp.zeros_like(out_ref)
+        total[...] = jnp.zeros_like(total)
 
     fine_cos, fine_sin = fine_ref[0], fine_ref[1]
     blocks = DEPTH // LANES
@@ -131,26 +141,28 @@
         sine = table[:, DEPTH + first : DEPTH + first + width]
         for window in range(2):
             real, imag = pol_ref[2 * window], pol_ref[2 * window + 1]
-            out_ref[:, window, 0, first : first + width] += dot(real, cosine) + dot(imag, sine)
-            out_ref[:, window, 1, first : first + width] += dot(imag, cosine) - dot(real, sine)
+            total[2 * window, :, first : first + width] += dot(real, cosine) + dot(imag, sine)
+            total[2 * window + 1, :, first : first + width] += dot(imag, cosine) - dot(real, sine)
+
+    @pl.when(pl.program_id(0) == pl.num_programs(0) - 1)
+    def _():
+        out_ref[...] = total[...].astype(BF16)
 
 
 def transform(pol, fine, coarse):
     _, count, stations = pol.shape
     block = math.gcd(count, 256)
     out = pl.pallas_call(
-        lambda p, f, c, o, t: transform_kernel(
-            p, f, c, o, t
-        ),
+        transform_kernel,
         grid=(count // block,),
         in_specs=[
             pl.BlockSpec((4, block, stations), lambda i: (0, i, 0)),
             pl.BlockSpec((2, block, LANES), lambda i: (0, i, 0)),
             pl.BlockSpec((block, coarse.shape[1]), lambda i: (i, 0)),
         ],
-        out_specs=pl.BlockSpec((stations, 2, 2, DEPTH), lambda i: (0, 0, 0, 0)),
-        out_shape=jax.ShapeDtypeStruct((stations, 2, 2, DEPTH), F32),
-        scratch_shapes=[pltpu.VMEM((block, 2 * DEPTH), BF16)],
+        out_specs=pl.BlockSpec((4, stations, DEPTH), lambda i: (0, 0, 0)),
+        out_shape=jax.ShapeDtypeStruct((4, stations, DEPTH), BF16),
+        scratch_shapes=[pltpu.VMEM((block, 2 * DEPTH), BF16), pltpu.VMEM((4, stations, DEPTH), F32)],
         compiler_params=pltpu.CompilerParams(vmem_limit_bytes=40 << 20),
         cost_estimate=pl.CostEstimate(
             flops=2 * count * 4 * stations * 2 * DEPTH, bytes_accessed=16 << 20, transcendentals=0
@@ -268,6 +280,19 @@
         running = lax.ppermute(running, axis, pairs)
         running = add(running, block_of(lax.rem(place + 2 * size - 1 - step, size)))
     return running
+
+
+def after(value, *others):
+    return lax.optimization_barrier((value, *others))[0]
+
+
+def exchange_sum(value, axis, size):
+    terms = [value]
+    for flip in range(1, size):
+        terms.append(lax.ppermute(value, axis, [(place, place ^ flip) for place in range(size)]))
+    while len(terms) > 1:
+        terms = [terms[index] + terms[index + 1] for index in range(0, len(terms), 2)]
+    return terms[0]
 
 
 def per_device(voltages, window_stations, channel_flags):
@@ -292,20 +317,37 @@
     per_chunk = per_y // CHUNKS
     per_z = per_chunk // num_z
     order = [lax.rem(place_y + 2 * num_y - 1 - step, num_y) for step in range(num_y)]
-    vis, pols, visited = {}, [], []
-    for step, y_block in enumerate(order):
-        for chunk in range(CHUNKS):
-            first = y_block * per_y + chunk * per_chunk
-            vis[step, chunk], pol = correlate(voltages, window_stations, first, per_chunk)
-            pols.append(pol)
-            visited.append(chan * local + first + jnp.arange(per_chunk, dtype=jnp.int32))
+    chosen = selectors(window_stations, times, voltages.shape[2], inputs)
+    pols, arrived = [], []
+    for chunk in range(CHUNKS):
+        part, pol = correlate(voltages, chosen, order[0] * per_y + chunk * per_chunk, per_chunk)
+        pols.append(pol)
+        arrived.append(lax.ppermute(part, "tm", y_pairs))
+    own = []
+    for y_block in order[1:]:
+        first = after(y_block * per_y, arrived[0], pols[CHUNKS - 1])
+        part, pol = correlate(voltages, chosen, first, per_y)
+        own.append(part)
+        pols.append(pol)
     weights = channel_flags.astype(F32)
+    by_y = lax.dynamic_slice_in_dim(weights, chan * local, local, 0).reshape(num_y, per_y)
+    local_flags = jnp.concatenate(
+        [lax.dynamic_index_in_dim(by_y, y_block, 0, keepdims=False) for y_block in order]
+    )
+    local_channels = chan * local + jnp.arange(per_y, dtype=jnp.int32)
+    visited = jnp.concatenate([local_channels + y_block * per_y for y_block in order])
+    fine, coarse = tables(visited, local_flags)
+    spectrum = transform(jnp.concatenate(pols, 1), fine, coarse)
 
     finished = []
     for chunk in range(CHUNKS):
-        running = vis[0, chunk]
-        for step in range(1, num_y):
-            running = add(lax.ppermute(running, "tm", y_pairs), vis[step, chunk])
+        running = arrived[chunk]
+        if finished:
+            running = after(running, finished[-1], spectrum)
+        for step, part in enumerate(own):
+            if step:
+                running = lax.ppermute(running, "tm", y_pairs)
+            running = add(running, part[:, chunk * per_chunk : (chunk + 1) * per_chunk])
         parts = running.reshape(6, num_z, per_z, inputs)
 
         def z_block(index, parts=parts):
@@ -319,29 +361,24 @@
         (1, 1, CHUNKS, 1, per_z),
     ).reshape(-1, 1)
 
-    by_y = lax.dynamic_slice_in_dim(weights, chan * local, local, 0).reshape(num_y, per_y)
-    local_flags = jnp.concatenate(
-        [lax.dynamic_index_in_dim(by_y, y_block, 0, keepdims=False) for y_block in order]
-    )
-    fine, coarse = tables(jnp.concatenate(visited), local_flags)
-    spectrum = transform(jnp.concatenate(pols, 1), fine, coarse)
-    own = stations // (tm_size * chan_size)
-    cube = spectrum.astype(BF16).reshape(num_z, num_y, num_x, CORES, own, 2, 2, DEPTH)
+    kept = stations // (tm_size * chan_size)
+    cube = spectrum.reshape(4, num_z, num_y, num_x, CORES, kept, DEPTH)
     for axis, pairs, place, size, dim in (
-        ("chan", core_pairs, core, CORES, 3),
-        ("chan", x_pairs, place_x, num_x, 2),
-        ("tm", y_pairs, place_y, num_y, 1),
-        ("tm", z_pairs, place_z, num_z, 0),
+        ("chan", core_pairs, core, CORES, 4),
+        ("chan", x_pairs, place_x, num_x, 3),
+        ("tm", y_pairs, place_y, num_y, 2),
+        ("tm", z_pairs, place_z, num_z, 1),
     ):
         def block_of(index, cube=cube, dim=dim):
             return lax.dynamic_index_in_dim(cube, index, dim, keepdims=False)
 
         cube = ring_sum(block_of, place, size, axis, pairs)
     norm_factor = 1.0 / math.sqrt(CHANNELS * times * tm_size)
-    rm_spectrum = (cube.astype(F32) * norm_factor).reshape(1, own, 2, 2, DEPTH)
+    rm_spectrum = jnp.swapaxes(cube.astype(F32) * norm_factor, 0, 1)
+    rm_spectrum = rm_spectrum.reshape(1, kept, 2, 2, DEPTH)
 
     stats = statistics(own_vis, own_flags).reshape(16, stations, 2)[:, :, 0]
-    stats = lax.psum(stats, ("chan", "tm")) / CHANNELS
+    stats = exchange_sum(exchange_sum(stats, "chan", chan_size), "tm", tm_size) / CHANNELS
     return (rm_spectrum, fit(stats, window_stations))
 
 

time: 438 us -> 288 us (0.66)
  waiting for transfers between devices: 191 us -> 112 us
  blocking collectives: 37.9 us -> 0 us
  Pallas kernels: 126 us -> 101 us
  local copies, waits for them, and re-layouts: 30.2 us -> 11.5 us
  starting transfers between devices: 25 us -> 31.4 us
  other arithmetic: 25.6 us -> 30.2 us
    ppermute x4 -> x14, waiting for transfers between devices: 70.6 us -> 11.9 us  [the longest x10 6.16 us: exchange_sum(): lax.ppermute(value, axis, [(place, place ^ flip) for place in range(size)])]
    psum x1 -> x0, blocking collectives: 37.9 us -> none  [per_device(): stats = lax.psum(stats, ('chan', 'tm')) / CHANNELS]
    ppermute x18, waiting for transfers between devices: 120 us -> 99.7 us  [ring_sum(): running = lax.ppermute(running, axis, pairs)]
    pallas_call x1, Pallas kernels: 34.2 us -> 16.9 us  [transform(): pl.pallas_call(transform_kernel, grid=(count // block,), in_specs=[pl.Blo...]
    ppermute x4 -> x14, starting transfers between devices: 4.57 us -> 19.3 us  [the longest x10 13.5 us: exchange_sum(): lax.ppermute(value, axis, [(place, place ^ flip) for place in range(size)])]
    unnamed x54 -> x41, local copies, waits for them, and re-layouts: 19.5 us -> 7.04 us
    ppermute x18, starting transfers between devices: 20.5 us -> 12.1 us  [ring_sum(): running = lax.ppermute(running, axis, pairs)]
    convert_element_type x21, other arithmetic: 13.9 us -> 22.1 us  [add(): return (left.astype(F32) + right.astype(F32)).astype(BF16)]
  transfers between devices with their start and end apart: 22 -> 32, of which waited for: 18 -> 16; matrix products, arithmetic and copies ran while one was open for 4% -> 10% of each run, Pallas kernels for 0% -> 31%
where the time goes in v2:
time: 288 us; the launch traced here: 287 us
  waiting for transfers between devices  112 us (39%)
  Pallas kernels  101 us (35%)
  starting transfers between devices  31.4 us (11%)
  other arithmetic  30.2 us (10%)
  local copies, waits for them, and re-layouts  11.5 us (4%)
    ppermute x18, waiting for transfers between devices, ring_sum(): running = lax.ppermute(running, axis, pairs)  99.7 us
    pallas_call x5, Pallas kernels, correlate(): pl.pallas_call(correlate_kernel, grid_spec=pltpu.PrefetchScalarGridSpec(n...  78.9 us
    convert_element_type x21, other arithmetic, add(): return (left.astype(F32) + right.astype(F32)).astype(BF16)  22.1 us
    pallas_call x1, Pallas kernels, transform(): pl.pallas_call(transform_kernel, grid=(count // block,), in_specs=[pl.Blo...  16.9 us
    ppermute x10, starting transfers between devices, exchange_sum(): lax.ppermute(value, axis, [(place, place ^ flip) for place in range(size)])  13.5 us
    ppermute x18, starting transfers between devices, ring_sum(): running = lax.ppermute(running, axis, pairs)  12.1 us
    unnamed x41, local copies, waits for them, and re-layouts  7.04 us
    ppermute x10, waiting for transfers between devices, exchange_sum(): lax.ppermute(value, axis, [(place, place ^ flip) for place in range(size)])  6.16 us
  transfers between devices with their start and end apart: 32, of which 16 were waited for; matrix products, arithmetic and copies ran while one was open for 10% of the time, Pallas kernels for 31%

profile of v2, /device:TPU:0, one launch (start us, length us, event | category | flops | bytes accessed | tf_op | source)
XLA Modules:
  0.0 287.0 jit_solution(14608887141405004025)
XLA Ops:
  2.3 10.7 %correlate.5 = (bf16[6,256,512]{2,1,0:T(8,128)(2,1)}, bf16[4,256,256]{2,1,0:T(8,128)(2,1)S(1)}) custom-call(s32[1]{0:T(128)} %bitcast.scalars, bf16[8,2048,2,512]{3,2,1,0:T(2,128)(2,1)} %x_ref.9, f32[3,256,128]{2,1,0:T(8,128)S(1)} %pad_maximum_fusion.2.mask_ref, bf16[512,128]{1,0:T(8,128)(2,1)S(1)} %fusion.16.pick_ref, bf16[512,256]{1,0:T(8,128)(2,1)S(1)} %fusion.15.pair_ref), custom_call_target="tpu_custom_call" | custom-call | flops 1073741824 | bytes 8388608 | tf_op jit(solution)/shard_map/correlate/pallas_call | solution.py:92
  13.0 3.0 %collective-permute-start = (bf16[6,256,512]{2,1,0:T(8,128)(2,1)}, bf16[6,256,512]{2,1,0:T(8,128)(2,1)}, u32[]{:S(2)}, u32[]{:S(2)}) collective-permute-start(bf16[6,256,512]{2,1,0:T(8,128)(2,1)} %get-tuple-element.20), channel_id=1, source_target_pairs={{0,1},{1,0},{2,3},{3,2},{4,5},{5,4},{6,7},{7,6},{8,9},{9,8},{10,11... | collective-permute-start | bytes 4718600 | tf_op jit(solution)/shard_map/ppermute | solution.py:325
  16.0 10.7 %correlate.6 = (bf16[6,256,512]{2,1,0:T(8,128)(2,1)}, bf16[4,256,256]{2,1,0:T(8,128)(2,1)S(1)}) custom-call(s32[1]{0:T(128)} %bitcast.1.scalars, bf16[8,2048,2,512]{3,2,1,0:T(2,128)(2,1)} %x_ref.9, f32[3,256,128]{2,1,0:T(8,128)S(1)} %pad_maximum_fusion.2.mask_ref, bf16[512,128]{1,0:T(8,128)(2,1)S(1)} %fusion.16.pick_ref, bf16[512,256]{1,0:T(8,128)(2,1)S(1)} %fusion.15.pair_ref), custom_call_target="tpu_custom_call" | custom-call | flops 1073741824 | bytes 8388608 | tf_op jit(solution)/shard_map/correlate/pallas_call | solution.py:92
  27.7 10.7 %correlate.8 = (bf16[6,256,512]{2,1,0:T(8,128)(2,1)}, bf16[4,256,256]{2,1,0:T(8,128)(2,1)S(1)}) custom-call(s32[1]{0:T(128)} %bitcast.3.scalars, bf16[8,2048,2,512]{3,2,1,0:T(2,128)(2,1)} %x_ref.9, f32[3,256,128]{2,1,0:T(8,128)S(1)} %pad_maximum_fusion.2.mask_ref, bf16[512,128]{1,0:T(8,128)(2,1)S(1)} %fusion.16.pick_ref, bf16[512,256]{1,0:T(8,128)(2,1)S(1)} %fusion.15.pair_ref), custom_call_target="tpu_custom_call" | custom-call | flops 1073741824 | bytes 8388608 | tf_op jit(solution)/shard_map/correlate/pallas_call | solution.py:92
  38.4 10.2 %correlate.7 = (bf16[6,256,512]{2,1,0:T(8,128)(2,1)S(1)}, bf16[4,256,256]{2,1,0:T(8,128)(2,1)S(1)}) custom-call(s32[1]{0:T(128)} %bitcast.2.scalars, bf16[8,2048,2,512]{3,2,1,0:T(2,128)(2,1)} %x_ref.9, f32[3,256,128]{2,1,0:T(8,128)S(1)} %pad_maximum_fusion.2.mask_ref, bf16[512,128]{1,0:T(8,128)(2,1)S(1)} %fusion.16.pick_ref, ...), custom_call_target="tpu_custom_call" | custom-call | flops 1073741824 | bytes 8388608 | tf_op jit(solution)/shard_map/correlate/pallas_call | solution.py:92
  49.6 5.5 %multiply_cosine_fusion = (f32[1,2048,128]{2,1,0:T(8,128)}, f32[1,2048,128]{2,1,0:T(8,128)}) fusion(f32[128]{0:T(128)S(1)} %convert_multiply_fusion.2, f32[2048]{0:T(1024)S(1)} %fusion.30), kind=kLoop, calls=%fused_computation.9 | loop fusion | flops 262144 | bytes 2105856 | tf_op jit(solution)/shard_map/cos | solution.py:180
  55.2 36.5 %correlate.9 = (bf16[6,1024,512]{2,1,0:T(8,128)(2,1)S(1)}, bf16[4,1024,256]{2,1,0:T(8,128)(2,1)S(1)}) custom-call(s32[1]{0:T(128)} %bitcast.4.scalars, bf16[8,2048,2,512]{3,2,1,0:T(2,128)(2,1)} %x_ref.9, f32[3,256,128]{2,1,0:T(8,128)S(1)} %pad_maximum_fusion.2.mask_ref, bf16[512,128]{1,0:T(8,128)(2,1)S(1)} %fusion.16.pick_ref, ...), custom_call_target="tpu_custom_call" | custom-call | flops 4294967296 | bytes 33554432 | tf_op jit(solution)/shard_map/correlate/pallas_call | solution.py:92
  91.7 3.2 %add_convert_fusion.3 = bf16[6,256,512]{2,1,0:T(8,128)(2,1)S(1)} fusion(bf16[6,256,512]{2,1,0:T(8,128)(2,1)} %collective-permute-done, bf16[6,1024,512]{2,1,0:T(8,128)(2,1)S(1)} %get-tuple-element.23), kind=kLoop, calls=%fused_computation.3 | loop fusion | flops 3145728 | bytes 4718592 | tf_op jit(solution)/shard_map/convert_element_type | solution.py:274
  95.0 2.1 collective-permute-start.7
  97.5 10.2 %collective-permute-done.7 = bf16[6,64,512]{2,1,0:T(8,128)(2,1)S(1)} collective-permute-done((bf16[6,64,512]{2,1,0:T(8,128)(2,1)S(1)}, bf16[6,64,512]{2,1,0:T(8,128)(2,1)S(1)}, u32[]{:S(2)}, u32[]{:S(2)}) %collective-permute-start.7) | collective-permute-done | bytes 393248 | tf_op jit(solution)/shard_map/ppermute | solution.py:280
  110.2 9.1 %collective-permute-done.8 = bf16[6,64,512]{2,1,0:T(8,128)(2,1)S(1)} collective-permute-done((bf16[6,64,512]{2,1,0:T(8,128)(2,1)S(1)}, bf16[6,64,512]{2,1,0:T(8,128)(2,1)S(1)}, u32[]{:S(2)}, u32[]{:S(2)}) %collective-permute-start.8) | collective-permute-done | bytes 393248 | tf_op jit(solution)/shard_map/ppermute | solution.py:280
  119.5 2.2 copy-done.7
  121.7 16.9 %transform.1 = bf16[4,256,1024]{2,1,0:T(8,128)(2,1)S(1)} custom-call(bf16[4,2048,256]{2,1,0:T(8,128)(2,1)S(1)} %copy-done.7, f32[2,2048,128]{2,1,0:T(8,128)S(1)} %pad_maximum_fusion.fine_ref, f32[2048,16]{1,0:T(8,128)S(1)} %bitcast.119), custom_call_target="tpu_custom_call" | custom-call | flops 8589934592 | bytes 16777216 | tf_op jit(solution)/shard_map/transform/pallas_call | solution.py:155
  142.2 9.2 %collective-permute-done.11 = bf16[6,64,512]{2,1,0:T(8,128)(2,1)S(1)} collective-permute-done((bf16[6,64,512]{2,1,0:T(8,128)(2,1)S(1)}, bf16[6,64,512]{2,1,0:T(8,128)(2,1)S(1)}, u32[]{:S(2)}, u32[]{:S(2)}) %collective-permute-start.11) | collective-permute-done | bytes 393248 | tf_op jit(solution)/shard_map/ppermute | solution.py:280
  151.6 9.6 %collective-permute-done.12 = bf16[6,64,512]{2,1,0:T(8,128)(2,1)S(1)} collective-permute-done((bf16[6,64,512]{2,1,0:T(8,128)(2,1)S(1)}, bf16[6,64,512]{2,1,0:T(8,128)(2,1)S(1)}, u32[]{:S(2)}, u32[]{:S(2)}) %collective-permute-start.12) | collective-permute-done | bytes 393248 | tf_op jit(solution)/shard_map/ppermute | solution.py:280
  161.4 9.6 %collective-permute-done.13 = bf16[6,64,512]{2,1,0:T(8,128)(2,1)S(1)} collective-permute-done((bf16[6,64,512]{2,1,0:T(8,128)(2,1)S(1)}, bf16[6,64,512]{2,1,0:T(8,128)(2,1)S(1)}, u32[]{:S(2)}, u32[]{:S(2)}) %collective-permute-start.13) | collective-permute-done | bytes 393248 | tf_op jit(solution)/shard_map/ppermute | solution.py:280
  171.8 3.1 %collective-permute-done.14 = bf16[6,256,512]{2,1,0:T(8,128)(2,1)S(1)} collective-permute-done((bf16[6,256,512]{2,1,0:T(8,128)(2,1)S(1)}, bf16[6,256,512]{2,1,0:T(8,128)(2,1)S(1)}, u32[]{:S(2)}, u32[]{:S(2)}) %collective-permute-start.14) | collective-permute-done | bytes 1572896 | tf_op jit(solution)/shard_map/ppermute | solution.py:325
  179.0 8.4 %collective-permute-done.15 = bf16[6,64,512]{2,1,0:T(8,128)(2,1)} collective-permute-done((bf16[6,64,512]{2,1,0:T(8,128)(2,1)}, bf16[6,64,512]{2,1,0:T(8,128)(2,1)}, u32[]{:S(2)}, u32[]{:S(2)}) %collective-permute-start.15) | collective-permute-done | bytes 393248 | tf_op jit(solution)/shard_map/ppermute | solution.py:280
  189.4 9.9 %collective-permute-done.16 = bf16[6,64,512]{2,1,0:T(8,128)(2,1)} collective-permute-done((bf16[6,64,512]{2,1,0:T(8,128)(2,1)}, bf16[6,64,512]{2,1,0:T(8,128)(2,1)}, u32[]{:S(2)}, u32[]{:S(2)}) %collective-permute-start.16) | collective-permute-done | bytes 393248 | tf_op jit(solution)/shard_map/ppermute | solution.py:280
  203.6 6.7 %collective-permute-done.17 = bf16[6,64,512]{2,1,0:T(8,128)(2,1)S(1)} collective-permute-done((bf16[6,64,512]{2,1,0:T(8,128)(2,1)S(1)}, bf16[6,64,512]{2,1,0:T(8,128)(2,1)S(1)}, u32[]{:S(2)}, u32[]{:S(2)}) %collective-permute-start.17) | collective-permute-done | bytes 393248 | tf_op jit(solution)/shard_map/ppermute | solution.py:280
  212.1 2.6 collective-permute-done.18
  214.8 2.3 add_convert_fusion
  217.9 4.3 %collective-permute-start.19 = (bf16[6,64,512]{2,1,0:T(8,128)(2,1)}, bf16[6,64,512]{2,1,0:T(8,128)(2,1)}, u32[]{:S(2)}, u32[]{:S(2)}) collective-permute-start(bf16[6,64,512]{2,1,0:T(8,128)(2,1)} %dynamic-slice_bitcast_fusion.2), channel_id=1, source_target_pairs={{0,2},{1,3},{2,4},{3,5},{4,6},{5,7},{6,0},{7,1},{8,10},{9,11},{10,... | collective-permute-start | bytes 1179656 | tf_op jit(solution)/shard_map/ppermute | solution.py:280
  224.6 6.4 %collective-permute-done.19 = bf16[6,64,512]{2,1,0:T(8,128)(2,1)} collective-permute-done((bf16[6,64,512]{2,1,0:T(8,128)(2,1)}, bf16[6,64,512]{2,1,0:T(8,128)(2,1)}, u32[]{:S(2)}, u32[]{:S(2)}) %collective-permute-start.19) | collective-permute-done | bytes 393248 | tf_op jit(solution)/shard_map/ppermute | solution.py:280
  232.1 2.3 collective-permute-start.20
  234.4 9.6 %collective-permute-done.20 = bf16[6,64,512]{2,1,0:T(8,128)(2,1)S(1)} collective-permute-done((bf16[6,64,512]{2,1,0:T(8,128)(2,1)S(1)}, bf16[6,64,512]{2,1,0:T(8,128)(2,1)S(1)}, u32[]{:S(2)}, u32[]{:S(2)}) %collective-permute-start.20) | collective-permute-done | bytes 393248 | tf_op jit(solution)/shard_map/ppermute | solution.py:280
  245.6 11.1 %collective-permute-done.4 = bf16[4,8,1024]{2,1,0:T(8,128)(2,1)} collective-permute-done((bf16[4,8,1024]{2,1,0:T(8,128)(2,1)}, bf16[4,8,1024]{2,1,0:T(8,128)(2,1)}, u32[]{:S(2)}, u32[]{:S(2)}) %collective-permute-start.4) | collective-permute-done | bytes 65568 | tf_op jit(solution)/shard_map/ppermute | solution.py:280
  259.4 3.6 %statistics.1 = f32[16,512]{1,0:T(8,128)S(1)} custom-call(bf16[6,256,512]{2,1,0:T(8,128)(2,1)S(1)} %pad_maximum_fusion.1.vis_ref, f32[256,1]{1,0:T(8,128)S(1)} %reshape.650.flag_ref), custom_call_target="tpu_custom_call" | custom-call | tf_op jit(solution)/shard_map/statistics/pallas_call | solution.py:215
  268.6 2.1 collective-permute-start.27
  270.7 3.4 %collective-permute-start.28 = (f32[16,256]{1,0:T(8,128)S(1)}, f32[16,256]{1,0:T(8,128)S(1)}, u32[]{:S(2)}, u32[]{:S(2)}) collective-permute-start(f32[16,256]{1,0:T(8,128)S(1)} %add_add_fusion), channel_id=1, source_target_pairs={{0,4},{1,5},{2,6},{3,7},{4,0},{5,1},{6,2},{7,3},{8,12},{9,13},{10,... | collective-permute-start | bytes 49160 | tf_op jit(solution)/shard_map/ppermute | solution.py:292
  274.5 3.8 %collective-permute-start.30 = (f32[16,256]{1,0:T(8,128)S(1)}, f32[16,256]{1,0:T(8,128)S(1)}, u32[]{:S(2)}, u32[]{:S(2)}) collective-permute-start(f32[16,256]{1,0:T(8,128)S(1)} %add_add_fusion), channel_id=1, source_target_pairs={{0,6},{1,7},{2,4},{3,5},{4,2},{5,3},{6,0},{7,1},{8,14},{9,15},{10,... | collective-permute-start | bytes 49160 | tf_op jit(solution)/shard_map/ppermute | solution.py:292
  280.2 4.6 %collective-permute-done.31 = f32[16,256]{1,0:T(8,128)S(1)} collective-permute-done((f32[16,256]{1,0:T(8,128)S(1)}, f32[16,256]{1,0:T(8,128)S(1)}, u32[]{:S(2)}, u32[]{:S(2)}) %collective-permute-start.31) | collective-permute-done | bytes 16416 | tf_op jit(solution)/shard_map/ppermute | solution.py:292
  (152 shorter events, 42.1 us)
Async XLA Ops:
  13.0 42.2 %collective-permute-start = (bf16[6,256,512]{2,1,0:T(8,128)(2,1)}, bf16[6,256,512]{2,1,0:T(8,128)(2,1)}, u32[]{:S(2)}, u32[]{:S(2)}) collective-permute-start(bf16[6,256,512]{2,1,0:T(8,128)(2,1)} %get-tuple-element.20), channel_id=1, source_target_pairs={{0,1},{1,0},{2,3},{3,2},{4,5},{5,4},{6,7},{7,6},{8,9},{9,8},{10,11... | collective-permute-start | bytes 4718600 | tf_op jit(solution)/shard_map/ppermute | solution.py:325
  26.6 112.1 %collective-permute-start.10 = (bf16[6,256,512]{2,1,0:T(8,128)(2,1)}, bf16[6,256,512]{2,1,0:T(8,128)(2,1)}, u32[]{:S(2)}, u32[]{:S(2)}) collective-permute-start(bf16[6,256,512]{2,1,0:T(8,128)(2,1)} %get-tuple-element.24), channel_id=1, source_target_pairs={{0,1},{1,0},{2,3},{3,2},{4,5},{5,4},{6,7},{7,6},{8,9},{9,8},{10,11... | collective-permute-start | bytes 4718600 | tf_op jit(solution)/shard_map/ppermute | solution.py:325
  95.0 12.7 %collective-permute-start.7 = (bf16[6,64,512]{2,1,0:T(8,128)(2,1)S(1)}, bf16[6,64,512]{2,1,0:T(8,128)(2,1)S(1)}, u32[]{:S(2)}, u32[]{:S(2)}) collective-permute-start(bf16[6,64,512]{2,1,0:T(8,128)(2,1)S(1)} %dynamic-slice_bitcast_fusion.5), channel_id=1, source_target_pairs={{0,2},{1,3},{2,4},{3,5},{4,6},{5,7},{6,0},{7,1},{8,10},{9,11},{10,... | collective-permute-start | bytes 1179656 | tf_op jit(solution)/shard_map/ppermute | solution.py:280
  107.8 11.5 %collective-permute-start.8 = (bf16[6,64,512]{2,1,0:T(8,128)(2,1)S(1)}, bf16[6,64,512]{2,1,0:T(8,128)(2,1)S(1)}, u32[]{:S(2)}, u32[]{:S(2)}) collective-permute-start(bf16[6,64,512]{2,1,0:T(8,128)(2,1)S(1)} %fusion.13), channel_id=1, source_target_pairs={{0,2},{1,3},{2,4},{3,5},{4,6},{5,7},{6,0},{7,1},{8,10},{9,11},{10,... | collective-permute-start | bytes 1179656 | tf_op jit(solution)/shard_map/ppermute | solution.py:280
  119.4 19.1 %collective-permute-start.9 = (bf16[6,64,512]{2,1,0:T(8,128)(2,1)S(1)}, bf16[6,64,512]{2,1,0:T(8,128)(2,1)S(1)}, u32[]{:S(2)}, u32[]{:S(2)}) collective-permute-start(bf16[6,64,512]{2,1,0:T(8,128)(2,1)S(1)} %fusion.12), channel_id=1, source_target_pairs={{0,2},{1,3},{2,4},{3,5},{4,6},{5,7},{6,0},{7,1},{8,10},{9,11},{10,... | collective-permute-start | bytes 1179656 | tf_op jit(solution)/shard_map/ppermute | solution.py:280
  140.8 10.6 %collective-permute-start.11 = (bf16[6,64,512]{2,1,0:T(8,128)(2,1)S(1)}, bf16[6,64,512]{2,1,0:T(8,128)(2,1)S(1)}, u32[]{:S(2)}, u32[]{:S(2)}) collective-permute-start(bf16[6,64,512]{2,1,0:T(8,128)(2,1)S(1)} %dynamic-slice_bitcast_fusion.4), channel_id=1, source_target_pairs={{0,2},{1,3},{2,4},{3,5},{4,6},{5,7},{6,0},{7,1},{8,10},{9,11},{10,... | collective-permute-start | bytes 1179656 | tf_op jit(solution)/shard_map/ppermute | solution.py:280
  140.9 34.1 %collective-permute-start.14 = (bf16[6,256,512]{2,1,0:T(8,128)(2,1)S(1)}, bf16[6,256,512]{2,1,0:T(8,128)(2,1)S(1)}, u32[]{:S(2)}, u32[]{:S(2)}) collective-permute-start(bf16[6,256,512]{2,1,0:T(8,128)(2,1)S(1)} %copy-done.9), channel_id=1, source_target_pairs={{0,1},{1,0},{2,3},{3,2},{4,5},{5,4},{6,7},{7,6},{8,9},{9,8},{10,11... | collective-permute-start | bytes 4718600 | tf_op jit(solution)/shard_map/ppermute | solution.py:325
  151.5 9.7 %collective-permute-start.12 = (bf16[6,64,512]{2,1,0:T(8,128)(2,1)S(1)}, bf16[6,64,512]{2,1,0:T(8,128)(2,1)S(1)}, u32[]{:S(2)}, u32[]{:S(2)}) collective-permute-start(bf16[6,64,512]{2,1,0:T(8,128)(2,1)S(1)} %fusion.10), channel_id=1, source_target_pairs={{0,2},{1,3},{2,4},{3,5},{4,6},{5,7},{6,0},{7,1},{8,10},{9,11},{10,... | collective-permute-start | bytes 1179656 | tf_op jit(solution)/shard_map/ppermute | solution.py:280
  161.3 9.6 %collective-permute-start.13 = (bf16[6,64,512]{2,1,0:T(8,128)(2,1)S(1)}, bf16[6,64,512]{2,1,0:T(8,128)(2,1)S(1)}, u32[]{:S(2)}, u32[]{:S(2)}) collective-permute-start(bf16[6,64,512]{2,1,0:T(8,128)(2,1)S(1)} %fusion.9), channel_id=1, source_target_pairs={{0,2},{1,3},{2,4},{3,5},{4,6},{5,7},{6,0},{7,1},{8,10},{9,11},{10,... | collective-permute-start | bytes 1179656 | tf_op jit(solution)/shard_map/ppermute | solution.py:280
  177.5 9.9 %collective-permute-start.15 = (bf16[6,64,512]{2,1,0:T(8,128)(2,1)}, bf16[6,64,512]{2,1,0:T(8,128)(2,1)}, u32[]{:S(2)}, u32[]{:S(2)}) collective-permute-start(bf16[6,64,512]{2,1,0:T(8,128)(2,1)} %dynamic-slice_bitcast_fusion.3), channel_id=1, source_target_pairs={{0,2},{1,3},{2,4},{3,5},{4,6},{5,7},{6,0},{7,1},{8,10},{9,11},{10,... | collective-permute-start | bytes 1179656 | tf_op jit(solution)/shard_map/ppermute | solution.py:280
  177.6 23.2 %collective-permute-start.1 = (bf16[4,4,2,2,8,1024]{5,4,3,2,1,0:T(8,128)(2,1)S(1)}, bf16[4,4,2,2,8,1024]{5,4,3,2,1,0:T(8,128)(2,1)}, u32[]{:S(2)}, u32[]{:S(2)}) collective-permute-start(bf16[4,4,2,2,8,1024]{5,4,3,2,1,0:T(8,128)(2,1)S(1)} %dynamic-slice_bitcast_fusion), channel_id=1, source_target_pairs={{0,8},{8,0},{16,24},{24,16},{1,9},{9,1},{17,25},{25,17},{2,10},{10... | collective-permute-start | bytes 3145736 | tf_op jit(solution)/shard_map/ppermute | solution.py:280
  177.6 37.1 %collective-permute-start.18 = (bf16[6,256,512]{2,1,0:T(8,128)(2,1)}, bf16[6,256,512]{2,1,0:T(8,128)(2,1)}, u32[]{:S(2)}, u32[]{:S(2)}) collective-permute-start(bf16[6,256,512]{2,1,0:T(8,128)(2,1)} %get-tuple-element.28), channel_id=1, source_target_pairs={{0,1},{1,0},{2,3},{3,2},{4,5},{5,4},{6,7},{7,6},{8,9},{9,8},{10,11... | collective-permute-start | bytes 4718600 | tf_op jit(solution)/shard_map/ppermute | solution.py:325
  189.4 9.9 %collective-permute-start.16 = (bf16[6,64,512]{2,1,0:T(8,128)(2,1)}, bf16[6,64,512]{2,1,0:T(8,128)(2,1)}, u32[]{:S(2)}, u32[]{:S(2)}) collective-permute-start(bf16[6,64,512]{2,1,0:T(8,128)(2,1)} %fusion.7), channel_id=1, source_target_pairs={{0,2},{1,3},{2,4},{3,5},{4,6},{5,7},{6,0},{7,1},{8,10},{9,11},{10,... | collective-permute-start | bytes 1179656 | tf_op jit(solution)/shard_map/ppermute | solution.py:280
  200.5 9.8 %collective-permute-start.17 = (bf16[6,64,512]{2,1,0:T(8,128)(2,1)S(1)}, bf16[6,64,512]{2,1,0:T(8,128)(2,1)S(1)}, u32[]{:S(2)}, u32[]{:S(2)}) collective-permute-start(bf16[6,64,512]{2,1,0:T(8,128)(2,1)S(1)} %fusion.6), channel_id=1, source_target_pairs={{0,2},{1,3},{2,4},{3,5},{4,6},{5,7},{6,0},{7,1},{8,10},{9,11},{10,... | collective-permute-start | bytes 1179656 | tf_op jit(solution)/shard_map/ppermute | solution.py:280
  202.4 19.7 %collective-permute-start.2 = (bf16[4,4,2,8,1024]{4,3,2,1,0:T(8,128)(2,1)S(1)}, bf16[4,4,2,8,1024]{4,3,2,1,0:T(8,128)(2,1)}, u32[]{:S(2)}, u32[]{:S(2)}) collective-permute-start(bf16[4,4,2,8,1024]{4,3,2,1,0:T(8,128)(2,1)S(1)} %dynamic-slice_bitcast_fusion.1), channel_id=1, source_target_pairs={{0,16},{8,24},{16,0},{24,8},{1,17},{9,25},{17,1},{25,9},{2,18},{10... | collective-permute-start | bytes 1572872 | tf_op jit(solution)/shard_map/ppermute | solution.py:280
  217.9 13.1 %collective-permute-start.19 = (bf16[6,64,512]{2,1,0:T(8,128)(2,1)}, bf16[6,64,512]{2,1,0:T(8,128)(2,1)}, u32[]{:S(2)}, u32[]{:S(2)}) collective-permute-start(bf16[6,64,512]{2,1,0:T(8,128)(2,1)} %dynamic-slice_bitcast_fusion.2), channel_id=1, source_target_pairs={{0,2},{1,3},{2,4},{3,5},{4,6},{5,7},{6,0},{7,1},{8,10},{9,11},{10,... | collective-permute-start | bytes 1179656 | tf_op jit(solution)/shard_map/ppermute | solution.py:280
  223.4 10.9 %collective-permute-start.3 = (bf16[4,4,8,1024]{3,2,1,0:T(8,128)(2,1)S(1)}, bf16[4,4,8,1024]{3,2,1,0:T(8,128)(2,1)S(1)}, u32[]{:S(2)}, u32[]{:S(2)}) collective-permute-start(bf16[4,4,8,1024]{3,2,1,0:T(8,128)(2,1)S(1)} %dynamic-slice_bitcast_fusion.6), channel_id=1, source_target_pairs={{0,1},{1,0},{2,3},{3,2},{4,5},{5,4},{6,7},{7,6},{8,9},{9,8},{10,11... | collective-permute-start | bytes 786440 | tf_op jit(solution)/shard_map/ppermute | solution.py:280
  232.1 11.9 %collective-permute-start.20 = (bf16[6,64,512]{2,1,0:T(8,128)(2,1)S(1)}, bf16[6,64,512]{2,1,0:T(8,128)(2,1)S(1)}, u32[]{:S(2)}, u32[]{:S(2)}) collective-permute-start(bf16[6,64,512]{2,1,0:T(8,128)(2,1)S(1)} %fusion.4), channel_id=1, source_target_pairs={{0,2},{1,3},{2,4},{3,5},{4,6},{5,7},{6,0},{7,1},{8,10},{9,11},{10,... | collective-permute-start | bytes 1179656 | tf_op jit(solution)/shard_map/ppermute | solution.py:280
  244.1 14.0 %collective-permute-start.21 = (bf16[6,64,512]{2,1,0:T(8,128)(2,1)S(1)}, bf16[6,64,512]{2,1,0:T(8,128)(2,1)}, u32[]{:S(2)}, u32[]{:S(2)}) collective-permute-start(bf16[6,64,512]{2,1,0:T(8,128)(2,1)S(1)} %fusion.3), channel_id=1, source_target_pairs={{0,2},{1,3},{2,4},{3,5},{4,6},{5,7},{6,0},{7,1},{8,10},{9,11},{10,... | collective-permute-start | bytes 1179656 | tf_op jit(solution)/shard_map/ppermute | solution.py:280
  244.9 11.7 %collective-permute-start.4 = (bf16[4,8,1024]{2,1,0:T(8,128)(2,1)}, bf16[4,8,1024]{2,1,0:T(8,128)(2,1)}, u32[]{:S(2)}, u32[]{:S(2)}) collective-permute-start(bf16[4,8,1024]{2,1,0:T(8,128)(2,1)} %dynamic-slice_bitcast_fusion.7), channel_id=1, source_target_pairs={{0,2},{1,3},{2,4},{3,5},{4,6},{5,7},{6,0},{7,1},{8,10},{9,11},{10,... | collective-permute-start | bytes 196616 | tf_op jit(solution)/shard_map/ppermute | solution.py:280
  258.1 7.1 %collective-permute-start.5 = (bf16[4,8,1024]{2,1,0:T(8,128)(2,1)}, bf16[4,8,1024]{2,1,0:T(8,128)(2,1)}, u32[]{:S(2)}, u32[]{:S(2)}) collective-permute-start(bf16[4,8,1024]{2,1,0:T(8,128)(2,1)} %fusion.21), channel_id=1, source_target_pairs={{0,2},{1,3},{2,4},{3,5},{4,6},{5,7},{6,0},{7,1},{8,10},{9,11},{10,... | collective-permute-start | bytes 196616 | tf_op jit(solution)/shard_map/ppermute | solution.py:280
  263.3 2.9 collective-permute-start.22
  263.4 3.8 %collective-permute-start.23 = (f32[16,256]{1,0:T(8,128)S(1)}, f32[16,256]{1,0:T(8,128)S(1)}, u32[]{:S(2)}, u32[]{:S(2)}) collective-permute-start(f32[16,256]{1,0:T(8,128)S(1)} %bitcast.139), channel_id=1, source_target_pairs={{0,16},{8,24},{16,0},{24,8},{1,17},{9,25},{17,1},{25,9},{2,18},{10... | collective-permute-start | bytes 49160 | tf_op jit(solution)/shard_map/ppermute | solution.py:292
  263.8 3.3 %collective-permute-start.24 = (f32[16,256]{1,0:T(8,128)S(1)}, f32[16,256]{1,0:T(8,128)S(1)}, u32[]{:S(2)}, u32[]{:S(2)}) collective-permute-start(f32[16,256]{1,0:T(8,128)S(1)} %bitcast.140), channel_id=1, source_target_pairs={{0,24},{8,16},{16,8},{24,0},{1,25},{9,17},{17,9},{25,1},{2,26},{10... | collective-permute-start | bytes 49160 | tf_op jit(solution)/shard_map/ppermute | solution.py:292
  266.1 8.0 %collective-permute-start.6 = (bf16[4,8,1024]{2,1,0:T(8,128)(2,1)S(1)}, bf16[4,8,1024]{2,1,0:T(8,128)(2,1)S(1)}, u32[]{:S(2)}, u32[]{:S(2)}) collective-permute-start(bf16[4,8,1024]{2,1,0:T(8,128)(2,1)S(1)} %fusion.20), channel_id=1, source_target_pairs={{0,2},{1,3},{2,4},{3,5},{4,6},{5,7},{6,0},{7,1},{8,10},{9,11},{10,... | collective-permute-start | bytes 196616 | tf_op jit(solution)/shard_map/ppermute | solution.py:280
  267.2 7.3 %collective-permute-start.25 = (f32[16,256]{1,0:T(8,128)S(1)}, f32[16,256]{1,0:T(8,128)S(1)}, u32[]{:S(2)}, u32[]{:S(2)}) collective-permute-start(f32[16,256]{1,0:T(8,128)S(1)} %add_add_fusion), channel_id=1, source_target_pairs={{0,1},{1,0},{2,3},{3,2},{4,5},{5,4},{6,7},{7,6},{8,9},{9,8},{10,11... | collective-permute-start | bytes 49160 | tf_op jit(solution)/shard_map/ppermute | solution.py:292
  268.6 9.7 %collective-permute-start.26 = (f32[16,256]{1,0:T(8,128)S(1)}, f32[16,256]{1,0:T(8,128)S(1)}, u32[]{:S(2)}, u32[]{:S(2)}) collective-permute-start(f32[16,256]{1,0:T(8,128)S(1)} %add_add_fusion), channel_id=1, source_target_pairs={{0,2},{1,3},{2,0},{3,1},{4,6},{5,7},{6,4},{7,5},{8,10},{9,11},{10,... | collective-permute-start | bytes 49160 | tf_op jit(solution)/shard_map/ppermute | solution.py:292
  268.6 11.0 %collective-permute-start.27 = (f32[16,256]{1,0:T(8,128)S(1)}, f32[16,256]{1,0:T(8,128)S(1)}, u32[]{:S(2)}, u32[]{:S(2)}) collective-permute-start(f32[16,256]{1,0:T(8,128)S(1)} %add_add_fusion), channel_id=1, source_target_pairs={{0,3},{1,2},{2,1},{3,0},{4,7},{5,6},{6,5},{7,4},{8,11},{9,10},{10,... | collective-permute-start | bytes 49160 | tf_op jit(solution)/shard_map/ppermute | solution.py:292
  270.7 8.9 %collective-permute-start.28 = (f32[16,256]{1,0:T(8,128)S(1)}, f32[16,256]{1,0:T(8,128)S(1)}, u32[]{:S(2)}, u32[]{:S(2)}) collective-permute-start(f32[16,256]{1,0:T(8,128)S(1)} %add_add_fusion), channel_id=1, source_target_pairs={{0,4},{1,5},{2,6},{3,7},{4,0},{5,1},{6,2},{7,3},{8,12},{9,13},{10,... | collective-permute-start | bytes 49160 | tf_op jit(solution)/shard_map/ppermute | solution.py:292
  274.1 5.5 %collective-permute-start.29 = (f32[16,256]{1,0:T(8,128)S(1)}, f32[16,256]{1,0:T(8,128)S(1)}, u32[]{:S(2)}, u32[]{:S(2)}) collective-permute-start(f32[16,256]{1,0:T(8,128)S(1)} %add_add_fusion), channel_id=1, source_target_pairs={{0,5},{1,4},{2,7},{3,6},{4,1},{5,0},{6,3},{7,2},{8,13},{9,12},{10,... | collective-permute-start | bytes 49160 | tf_op jit(solution)/shard_map/ppermute | solution.py:292
  274.5 5.7 %collective-permute-start.30 = (f32[16,256]{1,0:T(8,128)S(1)}, f32[16,256]{1,0:T(8,128)S(1)}, u32[]{:S(2)}, u32[]{:S(2)}) collective-permute-start(f32[16,256]{1,0:T(8,128)S(1)} %add_add_fusion), channel_id=1, source_target_pairs={{0,6},{1,7},{2,4},{3,5},{4,2},{5,3},{6,0},{7,1},{8,14},{9,15},{10,... | collective-permute-start | bytes 49160 | tf_op jit(solution)/shard_map/ppermute | solution.py:292
  278.3 6.4 %collective-permute-start.31 = (f32[16,256]{1,0:T(8,128)S(1)}, f32[16,256]{1,0:T(8,128)S(1)}, u32[]{:S(2)}, u32[]{:S(2)}) collective-permute-start(f32[16,256]{1,0:T(8,128)S(1)} %add_add_fusion), channel_id=1, source_target_pairs={{0,7},{1,6},{2,5},{3,4},{4,3},{5,2},{6,1},{7,0},{8,15},{9,14},{10,... | collective-permute-start | bytes 49160 | tf_op jit(solution)/shard_map/ppermute | solution.py:292
  (18 other events, 230.4 us)

commit v3 on v2

--- a/solution.py
+++ b/solution.py
@@ -14,7 +14,7 @@
 LANES = 128
 NUM_Z = 4
 CORES = 2
-CHUNKS = 4
+CHUNKS = (3, 3, 2)
 F32 = jnp.float32
 BF16 = jnp.bfloat16
 
@@ -110,9 +110,7 @@
             jax.ShapeDtypeStruct((4, count, inputs // 2), BF16),
         ],
         compiler_params=pltpu.CompilerParams(vmem_limit_bytes=40 << 20),
-        cost_estimate=pl.CostEstimate(
-            flops=count * 16 * 2 * 512 * 256, bytes_accessed=count * 16 * 1024 * 2, transcendentals=0
-        ),
+        cost_estimate=pl.CostEstimate(flops=1024, bytes_accessed=1024, transcendentals=0),
         name="correlate",
     )(scalars, voltages, *chosen)
 
@@ -164,9 +162,7 @@
         out_shape=jax.ShapeDtypeStruct((4, stations, DEPTH), BF16),
         scratch_shapes=[pltpu.VMEM((block, 2 * DEPTH), BF16), pltpu.VMEM((4, stations, DEPTH), F32)],
         compiler_params=pltpu.CompilerParams(vmem_limit_bytes=40 << 20),
-        cost_estimate=pl.CostEstimate(
-            flops=2 * count * 4 * stations * 2 * DEPTH, bytes_accessed=16 << 20, transcendentals=0
-        ),
+        cost_estimate=pl.CostEstimate(flops=1024, bytes_accessed=1024, transcendentals=0),
         name="transform",
     )(pol, fine, coarse)
     return out
@@ -274,10 +270,10 @@
     return (left.astype(F32) + right.astype(F32)).astype(BF16)
 
 
-def ring_sum(block_of, place, size, axis, pairs):
+def ring_sum(block_of, place, size, axis, pairs, before=()):
     running = block_of(lax.rem(place + size - 1, size))
     for step in range(1, size):
-        running = lax.ppermute(running, axis, pairs)
+        running = after(lax.ppermute(running, axis, pairs), *before)
         running = add(running, block_of(lax.rem(place + 2 * size - 1 - step, size)))
     return running
 
@@ -286,9 +282,9 @@
     return lax.optimization_barrier((value, *others))[0]
 
 
-def exchange_sum(value, axis, size):
+def exchange_sum(value, axis, size, unit, count):
     terms = [value]
-    for flip in range(1, size):
+    for flip in range(unit, unit * count, unit):
         terms.append(lax.ppermute(value, axis, [(place, place ^ flip) for place in range(size)]))
     while len(terms) > 1:
         terms = [terms[index] + terms[index + 1] for index in range(0, len(terms), 2)]
@@ -314,21 +310,24 @@
     core_pairs = [(x * CORES + c, x * CORES + (c + 1) % CORES) for x in range(num_x) for c in range(CORES)]
 
     per_y = local // num_y
-    per_chunk = per_y // CHUNKS
-    per_z = per_chunk // num_z
+    sizes = [share * per_y // sum(CHUNKS) for share in CHUNKS]
+    starts = [sum(sizes[:chunk]) for chunk in range(len(sizes))]
     order = [lax.rem(place_y + 2 * num_y - 1 - step, num_y) for step in range(num_y)]
     chosen = selectors(window_stations, times, voltages.shape[2], inputs)
     pols, arrived = [], []
-    for chunk in range(CHUNKS):
-        part, pol = correlate(voltages, chosen, order[0] * per_y + chunk * per_chunk, per_chunk)
+    for start, size in zip(starts, sizes):
+        part, pol = correlate(voltages, chosen, order[0] * per_y + start, size)
         pols.append(pol)
         arrived.append(lax.ppermute(part, "tm", y_pairs))
     own = []
     for y_block in order[1:]:
-        first = after(y_block * per_y, arrived[0], pols[CHUNKS - 1])
-        part, pol = correlate(voltages, chosen, first, per_y)
-        own.append(part)
-        pols.append(pol)
+        pieces = []
+        for chunk, (start, size) in enumerate(zip(starts, sizes)):
+            first = after(y_block * per_y + start, pols[len(sizes) - 1], *arrived[: min(chunk, 1)])
+            part, pol = correlate(voltages, chosen, first, size)
+            pieces.append(part)
+            pols.append(pol)
+        own.append(pieces)
     weights = channel_flags.astype(F32)
     by_y = lax.dynamic_slice_in_dim(weights, chan * local, local, 0).reshape(num_y, per_y)
     local_flags = jnp.concatenate(
@@ -337,28 +336,33 @@
     local_channels = chan * local + jnp.arange(per_y, dtype=jnp.int32)
     visited = jnp.concatenate([local_channels + y_block * per_y for y_block in order])
     fine, coarse = tables(visited, local_flags)
-    spectrum = transform(jnp.concatenate(pols, 1), fine, coarse)
 
     finished = []
-    for chunk in range(CHUNKS):
+    for chunk, size in enumerate(sizes):
         running = arrived[chunk]
         if finished:
-            running = after(running, finished[-1], spectrum)
+            running = after(running, finished[0])
         for step, part in enumerate(own):
             if step:
                 running = lax.ppermute(running, "tm", y_pairs)
-            running = add(running, part[:, chunk * per_chunk : (chunk + 1) * per_chunk])
-        parts = running.reshape(6, num_z, per_z, inputs)
+            running = add(running, part[chunk])
+        parts = running.reshape(6, num_z, size // num_z, inputs)
 
         def z_block(index, parts=parts):
             return lax.dynamic_index_in_dim(parts, index, 1, keepdims=False)
 
-        finished.append(ring_sum(z_block, place_z, num_z, "tm", z_pairs))
+        before = (arrived[2],) if chunk == 1 else ()
+        finished.append(ring_sum(z_block, place_z, num_z, "tm", z_pairs, before))
+    spectrum = transform(after(jnp.concatenate(pols, 1), arrived[2], finished[0]), fine, coarse)
     own_vis = jnp.concatenate(finished, 1)
-    own_flags = lax.dynamic_slice(
-        weights.reshape(chan_size, num_y, CHUNKS, num_z, per_z),
-        (chan, place_y, 0, place_z, 0),
-        (1, 1, CHUNKS, 1, per_z),
+    own_first = chan * local + place_y * per_y
+    own_flags = jnp.concatenate(
+        [
+            lax.dynamic_slice_in_dim(
+                weights, own_first + start + place_z * (size // num_z), size // num_z
+            )
+            for start, size in zip(starts, sizes)
+        ]
     ).reshape(-1, 1)
 
     kept = stations // (tm_size * chan_size)
@@ -378,7 +382,9 @@
     rm_spectrum = rm_spectrum.reshape(1, kept, 2, 2, DEPTH)
 
     stats = statistics(own_vis, own_flags).reshape(16, stations, 2)[:, :, 0]
-    stats = exchange_sum(exchange_sum(stats, "chan", chan_size), "tm", tm_size) / CHANNELS
+    stats = exchange_sum(stats, "chan", chan_size, 1, chan_size)
+    stats = exchange_sum(stats, "tm", tm_size, 1, num_y)
+    stats = exchange_sum(stats, "tm", tm_size, num_y, num_z) / CHANNELS
     return (rm_spectrum, fit(stats, window_stations))
 
 

time: 288 us -> 271 us (0.941)
  waiting for transfers between devices: 112 us -> 92 us
  starting transfers between devices: 31.4 us -> 25.4 us
  local copies, waits for them, and re-layouts: 11.5 us -> 17 us
    ppermute x18 -> x15, waiting for transfers between devices: 99.7 us -> 71.3 us  [ring_sum(): running = after(lax.ppermute(running, axis, pairs), *before)]
    ppermute x4 -> x3, waiting for transfers between devices: 5.78 us -> 12.1 us  [per_device(): arrived.append(lax.ppermute(part, 'tm', y_pairs))]
    unnamed x41 -> x40, local copies, waits for them, and re-layouts: 7.04 us -> 13.1 us
    ppermute x10 -> x7, starting transfers between devices: 13.5 us -> 7.87 us  [exchange_sum(): lax.ppermute(value, axis, [(place, place ^ flip) for place in range(size)])]
    ppermute x10 -> x7, waiting for transfers between devices: 6.16 us -> 8.56 us  [exchange_sum(): lax.ppermute(value, axis, [(place, place ^ flip) for place in range(size)])]
    pallas_call x5 -> x6, Pallas kernels: 78.9 us -> 79.8 us  [correlate(): pl.pallas_call(correlate_kernel, grid_spec=pltpu.PrefetchScalarGridSpec(n...]
    convert_element_type x21 -> x17, other arithmetic: 22.1 us -> 21.3 us  [add(): return (left.astype(F32) + right.astype(F32)).astype(BF16)]
    ppermute x18 -> x15, starting transfers between devices: 12.1 us -> 12.5 us  [ring_sum(): running = after(lax.ppermute(running, axis, pairs), *before)]
  transfers between devices with their start and end apart: 32 -> 25, of which waited for: 16 -> 14; matrix products, arithmetic and copies ran while one was open for 10% -> 14% of each run, Pallas kernels for 31% -> 32%
where the time goes in v3:
time: 271 us
  Pallas kernels  103 us (38%)
  waiting for transfers between devices  92 us (34%)
  other arithmetic  32.3 us (12%)
  starting transfers between devices  25.4 us (9%)
  local copies, waits for them, and re-layouts  17 us (6%)
    pallas_call x6, Pallas kernels, correlate(): pl.pallas_call(correlate_kernel, grid_spec=pltpu.PrefetchScalarGridSpec(n...  79.8 us
    ppermute x15, waiting for transfers between devices, ring_sum(): running = after(lax.ppermute(running, axis, pairs), *before)  71.3 us
    convert_element_type x17, other arithmetic, add(): return (left.astype(F32) + right.astype(F32)).astype(BF16)  21.3 us
    pallas_call x1, Pallas kernels, transform(): pl.pallas_call(transform_kernel, grid=(count // block,), in_specs=[pl.Blo...  17.8 us
    unnamed x40, local copies, waits for them, and re-layouts  13.1 us
    ppermute x15, starting transfers between devices, ring_sum(): running = after(lax.ppermute(running, axis, pairs), *before)  12.5 us
    ppermute x3, waiting for transfers between devices, per_device(): arrived.append(lax.ppermute(part, 'tm', y_pairs))  12.1 us
    ppermute x7, waiting for transfers between devices, exchange_sum(): lax.ppermute(value, axis, [(place, place ^ flip) for place in range(size)])  8.56 us
  transfers between devices with their start and end apart: 25, of which 14 were waited for; matrix products, arithmetic and copies ran while one was open for 14% of the time, Pallas kernels for 32%

profile of v3, /device:TPU:0, one launch (start us, length us, event | category | flops | bytes accessed | tf_op | source)
XLA Modules:
  0.0 270.6 jit_solution(5388610260460660926)
XLA Ops:
  2.3 15.1 %correlate.6 = (bf16[6,384,512]{2,1,0:T(8,128)(2,1)}, bf16[4,384,256]{2,1,0:T(8,128)(2,1)S(1)}) custom-call(s32[1]{0:T(128)} %bitcast.scalars, bf16[8,2048,2,512]{3,2,1,0:T(2,128)(2,1)} %x_ref.11, f32[3,256,128]{2,1,0:T(8,128)S(1)} %pad_maximum_fusion.2.mask_ref, bf16[512,128]{1,0:T(8,128)(2,1)S(1)} %fusion.13.pick_ref, bf16[512,256]{1,0:T(8,128)(2,1)S(1)} %fusion.12.pair_ref), custom_call_target="tpu_custom_call" | custom-call | flops 1024 | bytes 1024 | tf_op jit(solution)/shard_map/correlate/pallas_call | solution.py:92
  18.3 3.0 %collective-permute-start = (bf16[6,384,512]{2,1,0:T(8,128)(2,1)}, bf16[6,384,512]{2,1,0:T(8,128)(2,1)}, u32[]{:S(2)}, u32[]{:S(2)}) collective-permute-start(bf16[6,384,512]{2,1,0:T(8,128)(2,1)} %get-tuple-element.28), channel_id=1, source_target_pairs={{0,1},{1,0},{2,3},{3,2},{4,5},{5,4},{6,7},{7,6},{8,9},{9,8},{10,11... | collective-permute-start | bytes 7077896 | tf_op jit(solution)/shard_map/ppermute | solution.py:321
  21.2 15.1 %correlate.7 = (bf16[6,384,512]{2,1,0:T(8,128)(2,1)}, bf16[4,384,256]{2,1,0:T(8,128)(2,1)S(1)}) custom-call(s32[1]{0:T(128)} %bitcast.1.scalars, bf16[8,2048,2,512]{3,2,1,0:T(2,128)(2,1)} %x_ref.11, f32[3,256,128]{2,1,0:T(8,128)S(1)} %pad_maximum_fusion.2.mask_ref, bf16[512,128]{1,0:T(8,128)(2,1)S(1)} %fusion.13.pick_ref, bf16[512,256]{1,0:T(8,128)(2,1)S(1)} %fusion.12.pair_ref), custom_call_target="tpu_custom_call" | custom-call | flops 1024 | bytes 1024 | tf_op jit(solution)/shard_map/correlate/pallas_call | solution.py:92
  37.2 10.7 %correlate.8 = (bf16[6,256,512]{2,1,0:T(8,128)(2,1)}, bf16[4,256,256]{2,1,0:T(8,128)(2,1)S(1)}) custom-call(s32[1]{0:T(128)} %bitcast.2.scalars, bf16[8,2048,2,512]{3,2,1,0:T(2,128)(2,1)} %x_ref.11, f32[3,256,128]{2,1,0:T(8,128)S(1)} %pad_maximum_fusion.2.mask_ref, bf16[512,128]{1,0:T(8,128)(2,1)S(1)} %fusion.13.pick_ref, bf16[512,256]{1,0:T(8,128)(2,1)S(1)} %fusion.12.pair_ref), custom_call_target="tpu_custom_call" | custom-call | flops 1024 | bytes 1024 | tf_op jit(solution)/shard_map/correlate/pallas_call | solution.py:92
  48.7 2.0 collective-permute-start.1
  50.7 14.5 %correlate.9 = (bf16[6,384,512]{2,1,0:T(8,128)(2,1)S(1)}, bf16[4,384,256]{2,1,0:T(8,128)(2,1)S(1)}) custom-call(s32[1]{0:T(128)} %bitcast.3.scalars, bf16[8,2048,2,512]{3,2,1,0:T(2,128)(2,1)} %x_ref.11, f32[3,256,128]{2,1,0:T(8,128)S(1)} %pad_maximum_fusion.2.mask_ref, bf16[512,128]{1,0:T(8,128)(2,1)S(1)} %fusion.13.pick_ref, ...), custom_call_target="tpu_custom_call" | custom-call | flops 1024 | bytes 1024 | tf_op jit(solution)/shard_map/correlate/pallas_call | solution.py:92
  66.2 2.1 constant_dynamic-update-slice_fusion.5
  68.3 5.5 %multiply_cosine_fusion = (f32[1,2048,128]{2,1,0:T(8,128)}, f32[1,2048,128]{2,1,0:T(8,128)}) fusion(f32[128]{0:T(128)S(1)} %convert_multiply_fusion.2, f32[2048]{0:T(1024)S(1)} %fusion.27), kind=kLoop, calls=%fused_computation.8 | loop fusion | flops 262144 | bytes 2105856 | tf_op jit(solution)/shard_map/cos | solution.py:176
  73.8 2.4 add_convert_fusion.1
  76.3 2.0 collective-permute-start.2
  79.6 12.8 %collective-permute-done.2 = bf16[6,96,512]{2,1,0:T(8,128)(2,1)S(1)} collective-permute-done((bf16[6,96,512]{2,1,0:T(8,128)(2,1)S(1)}, bf16[6,96,512]{2,1,0:T(8,128)(2,1)S(1)}, u32[]{:S(2)}, u32[]{:S(2)}) %collective-permute-start.2) | collective-permute-done | bytes 589856 | tf_op jit(solution)/shard_map/ppermute | solution.py:276
  93.5 14.1 %collective-permute-done.3 = bf16[6,96,512]{2,1,0:T(8,128)(2,1)S(1)} collective-permute-done((bf16[6,96,512]{2,1,0:T(8,128)(2,1)S(1)}, bf16[6,96,512]{2,1,0:T(8,128)(2,1)S(1)}, u32[]{:S(2)}, u32[]{:S(2)}) %collective-permute-start.3) | collective-permute-done | bytes 589856 | tf_op jit(solution)/shard_map/ppermute | solution.py:276
  107.7 2.1 fusion.5
  111.0 3.0 %pad_maximum_fusion.fine_ref = f32[2,2048,128]{2,1,0:T(8,128)} fusion(f32[1,2048,128]{2,1,0:T(8,128)} %get-tuple-element.49, f32[1,2048,128]{2,1,0:T(8,128)} %get-tuple-element.48), kind=kLoop, calls=%fused_computation.3 | loop fusion | flops 524288 | bytes 4194304 | tf_op jit(solution)/shard_map/stack | solution.py:176
  114.0 14.5 %correlate.10 = (bf16[6,384,512]{2,1,0:T(8,128)(2,1)S(1)}, bf16[4,384,256]{2,1,0:T(8,128)(2,1)S(1)}) custom-call(s32[1]{0:T(128)} %bitcast.4.scalars, bf16[8,2048,2,512]{3,2,1,0:T(2,128)(2,1)} %x_ref.11, f32[3,256,128]{2,1,0:T(8,128)S(1)} %pad_maximum_fusion.2.mask_ref, bf16[512,128]{1,0:T(8,128)(2,1)S(1)} %fusion.13.pick_ref, ...), custom_call_target="tpu_custom_call" | custom-call | flops 1024 | bytes 1024 | tf_op jit(solution)/shard_map/correlate/pallas_call | solution.py:92
  130.8 10.1 %correlate.11 = (bf16[6,256,512]{2,1,0:T(8,128)(2,1)S(1)}, bf16[4,256,256]{2,1,0:T(8,128)(2,1)S(1)}) custom-call(s32[1]{0:T(128)} %bitcast.5.scalars, bf16[8,2048,2,512]{3,2,1,0:T(2,128)(2,1)} %x_ref.11, f32[3,256,128]{2,1,0:T(8,128)S(1)} %pad_maximum_fusion.2.mask_ref, bf16[512,128]{1,0:T(8,128)(2,1)S(1)} %fusion.13.pick_ref, ...), custom_call_target="tpu_custom_call" | custom-call | flops 1024 | bytes 1024 | tf_op jit(solution)/shard_map/correlate/pallas_call | solution.py:92
  142.7 2.3 fusion.4
  145.0 12.1 %collective-permute-done.1 = bf16[6,256,512]{2,1,0:T(8,128)(2,1)} collective-permute-done((bf16[6,256,512]{2,1,0:T(8,128)(2,1)}, bf16[6,256,512]{2,1,0:T(8,128)(2,1)}, u32[]{:S(2)}, u32[]{:S(2)}) %collective-permute-start.1) | collective-permute-done | bytes 1572896 | tf_op jit(solution)/shard_map/ppermute | solution.py:321
  157.1 2.0 add_convert_fusion.2
  159.1 2.0 collective-permute-start.15
  161.1 17.8 %transform.1 = bf16[4,256,1024]{2,1,0:T(8,128)(2,1)S(1)} custom-call(bf16[4,2048,256]{2,1,0:T(8,128)(2,1)} %constant_dynamic-update-slice_fusion.pol_ref, f32[2,2048,128]{2,1,0:T(8,128)S(1)} %copy-done, f32[2048,16]{1,0:T(8,128)S(1)} %bitcast.103), custom_call_target="tpu_custom_call" | custom-call | flops 1024 | bytes 1024 | tf_op jit(solution)/shard_map/transform/pallas_call | solution.py:153
  179.1 2.4 add_convert_fusion
  187.9 14.2 %collective-permute-done.12 = bf16[6,96,512]{2,1,0:T(8,128)(2,1)} collective-permute-done((bf16[6,96,512]{2,1,0:T(8,128)(2,1)}, bf16[6,96,512]{2,1,0:T(8,128)(2,1)}, u32[]{:S(2)}, u32[]{:S(2)}) %collective-permute-start.12) | collective-permute-done | bytes 589856 | tf_op jit(solution)/shard_map/ppermute | solution.py:276
  202.1 2.3 fusion.3
  204.4 6.2 %collective-permute-done.16 = bf16[6,64,512]{2,1,0:T(8,128)(2,1)} collective-permute-done((bf16[6,64,512]{2,1,0:T(8,128)(2,1)}, bf16[6,64,512]{2,1,0:T(8,128)(2,1)}, u32[]{:S(2)}, u32[]{:S(2)}) %collective-permute-start.16) | collective-permute-done | bytes 393248 | tf_op jit(solution)/shard_map/ppermute | solution.py:276
  215.5 7.7 %collective-permute-done.13 = bf16[6,96,512]{2,1,0:T(8,128)(2,1)} collective-permute-done((bf16[6,96,512]{2,1,0:T(8,128)(2,1)}, bf16[6,96,512]{2,1,0:T(8,128)(2,1)}, u32[]{:S(2)}, u32[]{:S(2)}) %collective-permute-start.13) | collective-permute-done | bytes 589856 | tf_op jit(solution)/shard_map/ppermute | solution.py:276
  224.6 6.9 %collective-permute-done.17 = bf16[6,64,512]{2,1,0:T(8,128)(2,1)S(1)} collective-permute-done((bf16[6,64,512]{2,1,0:T(8,128)(2,1)S(1)}, bf16[6,64,512]{2,1,0:T(8,128)(2,1)S(1)}, u32[]{:S(2)}, u32[]{:S(2)}) %collective-permute-start.17) | collective-permute-done | bytes 393248 | tf_op jit(solution)/shard_map/ppermute | solution.py:276
  234.4 9.3 %collective-permute-done.14 = bf16[6,96,512]{2,1,0:T(8,128)(2,1)S(1)} collective-permute-done((bf16[6,96,512]{2,1,0:T(8,128)(2,1)S(1)}, bf16[6,96,512]{2,1,0:T(8,128)(2,1)S(1)}, u32[]{:S(2)}, u32[]{:S(2)}) %collective-permute-start.14) | collective-permute-done | bytes 589856 | tf_op jit(solution)/shard_map/ppermute | solution.py:276
  245.2 3.6 %statistics.1 = f32[16,512]{1,0:T(8,128)S(1)} custom-call(bf16[6,256,512]{2,1,0:T(8,128)(2,1)S(1)} %pad_maximum_fusion.1.vis_ref, f32[256,1]{1,0:T(8,128)S(1)} %copy.53.flag_ref), custom_call_target="tpu_custom_call" | custom-call | tf_op jit(solution)/shard_map/statistics/pallas_call | solution.py:211
  255.5 2.2 collective-permute-done.21
  259.0 3.0 %collective-permute-start.23 = (f32[16,256]{1,0:T(8,128)S(1)}, f32[16,256]{1,0:T(8,128)S(1)}, u32[]{:S(2)}, u32[]{:S(2)}) collective-permute-start(f32[16,256]{1,0:T(8,128)S(1)} %add.440), channel_id=1, source_target_pairs={{0,4},{1,5},{2,6},{3,7},{4,0},{5,1},{6,2},{7,3},{8,12},{9,13},{10,... | collective-permute-start | bytes 49160 | tf_op jit(solution)/shard_map/ppermute | solution.py:288
  263.9 3.6 %collective-permute-done.24 = f32[16,256]{1,0:T(8,128)S(1)} collective-permute-done((f32[16,256]{1,0:T(8,128)S(1)}, f32[16,256]{1,0:T(8,128)S(1)}, u32[]{:S(2)}, u32[]{:S(2)}) %collective-permute-start.24) | collective-permute-done | bytes 16416 | tf_op jit(solution)/shard_map/ppermute | solution.py:288
  (135 shorter events, 43.0 us)
Async XLA Ops:
  18.3 55.5 %collective-permute-start = (bf16[6,384,512]{2,1,0:T(8,128)(2,1)}, bf16[6,384,512]{2,1,0:T(8,128)(2,1)}, u32[]{:S(2)}, u32[]{:S(2)}) collective-permute-start(bf16[6,384,512]{2,1,0:T(8,128)(2,1)} %get-tuple-element.28), channel_id=1, source_target_pairs={{0,1},{1,0},{2,3},{3,2},{4,5},{5,4},{6,7},{7,6},{8,9},{9,8},{10,11... | collective-permute-start | bytes 7077896 | tf_op jit(solution)/shard_map/ppermute | solution.py:321
  37.2 107.8 %collective-permute-start.11 = (bf16[6,384,512]{2,1,0:T(8,128)(2,1)}, bf16[6,384,512]{2,1,0:T(8,128)(2,1)}, u32[]{:S(2)}, u32[]{:S(2)}) collective-permute-start(bf16[6,384,512]{2,1,0:T(8,128)(2,1)} %get-tuple-element.36), channel_id=1, source_target_pairs={{0,1},{1,0},{2,3},{3,2},{4,5},{5,4},{6,7},{7,6},{8,9},{9,8},{10,11... | collective-permute-start | bytes 7077896 | tf_op jit(solution)/shard_map/ppermute | solution.py:321
  48.7 108.4 %collective-permute-start.1 = (bf16[6,256,512]{2,1,0:T(8,128)(2,1)}, bf16[6,256,512]{2,1,0:T(8,128)(2,1)}, u32[]{:S(2)}, u32[]{:S(2)}) collective-permute-start(bf16[6,256,512]{2,1,0:T(8,128)(2,1)} %get-tuple-element.33), channel_id=1, source_target_pairs={{0,1},{1,0},{2,3},{3,2},{4,5},{5,4},{6,7},{7,6},{8,9},{9,8},{10,11... | collective-permute-start | bytes 4718600 | tf_op jit(solution)/shard_map/ppermute | solution.py:321
  50.7 15.4 %copy-start.16 = (s32[8192]{0:T(1024)S(1)}, s32[8192]{0:T(1024)}, u32[]{:S(2)}) copy-start(s32[8192]{0:T(1024)} %param.5) | copy-start | bytes 98308
  76.2 16.2 %copy-start.13 = (bf16[6,384,512]{2,1,0:T(8,128)(2,1)}, bf16[6,384,512]{2,1,0:T(8,128)(2,1)S(1)}, u32[]{:S(2)}) copy-start(bf16[6,384,512]{2,1,0:T(8,128)(2,1)S(1)} %add_convert_fusion.1) | copy-start | bytes 7077892
  76.2 16.5 %copy-start.11 = (bf16[4,256,256]{2,1,0:T(8,128)(2,1)S(1)}, bf16[4,256,256]{2,1,0:T(8,128)(2,1)}, u32[]{:S(2)}) copy-start(bf16[4,256,256]{2,1,0:T(8,128)(2,1)} %copy-done.10) | copy-start | bytes 1572868
  76.3 16.1 %collective-permute-start.2 = (bf16[6,96,512]{2,1,0:T(8,128)(2,1)S(1)}, bf16[6,96,512]{2,1,0:T(8,128)(2,1)S(1)}, u32[]{:S(2)}, u32[]{:S(2)}) collective-permute-start(bf16[6,96,512]{2,1,0:T(8,128)(2,1)S(1)} %dynamic-slice_bitcast_fusion.2), channel_id=1, source_target_pairs={{0,2},{1,3},{2,4},{3,5},{4,6},{5,7},{6,0},{7,1},{8,10},{9,11},{10,... | collective-permute-start | bytes 1769480 | tf_op jit(solution)/shard_map/ppermute | solution.py:276
  79.6 30.1 %copy-start.6 = (bf16[4,384,256]{2,1,0:T(8,128)(2,1)S(1)}, bf16[4,384,256]{2,1,0:T(8,128)(2,1)}, u32[]{:S(2)}) copy-start(bf16[4,384,256]{2,1,0:T(8,128)(2,1)} %copy-done.5) | copy-start | bytes 2359300
  92.6 15.1 %collective-permute-start.3 = (bf16[6,96,512]{2,1,0:T(8,128)(2,1)S(1)}, bf16[6,96,512]{2,1,0:T(8,128)(2,1)S(1)}, u32[]{:S(2)}, u32[]{:S(2)}) collective-permute-start(bf16[6,96,512]{2,1,0:T(8,128)(2,1)S(1)} %fusion.6), channel_id=1, source_target_pairs={{0,2},{1,3},{2,4},{3,5},{4,6},{5,7},{6,0},{7,1},{8,10},{9,11},{10,... | collective-permute-start | bytes 1769480 | tf_op jit(solution)/shard_map/ppermute | solution.py:276
  109.7 32.9 %collective-permute-start.4 = (bf16[6,96,512]{2,1,0:T(8,128)(2,1)}, bf16[6,96,512]{2,1,0:T(8,128)(2,1)}, u32[]{:S(2)}, u32[]{:S(2)}) collective-permute-start(bf16[6,96,512]{2,1,0:T(8,128)(2,1)} %fusion.5), channel_id=1, source_target_pairs={{0,2},{1,3},{2,4},{3,5},{4,6},{5,7},{6,0},{7,1},{8,10},{9,11},{10,... | collective-permute-start | bytes 1769480 | tf_op jit(solution)/shard_map/ppermute | solution.py:276
  159.1 26.4 %copy-start.14 = (bf16[6,256,512]{2,1,0:T(8,128)(2,1)}, bf16[6,256,512]{2,1,0:T(8,128)(2,1)S(1)}, u32[]{:S(2)}) copy-start(bf16[6,256,512]{2,1,0:T(8,128)(2,1)S(1)} %add_convert_fusion.2) | copy-start | bytes 4718596
  159.1 26.3 %collective-permute-start.15 = (bf16[6,64,512]{2,1,0:T(8,128)(2,1)S(1)}, bf16[6,64,512]{2,1,0:T(8,128)(2,1)S(1)}, u32[]{:S(2)}, u32[]{:S(2)}) collective-permute-start(bf16[6,64,512]{2,1,0:T(8,128)(2,1)S(1)} %dynamic-slice_bitcast_fusion.4), channel_id=1, source_target_pairs={{0,2},{1,3},{2,4},{3,5},{4,6},{5,7},{6,0},{7,1},{8,10},{9,11},{10,... | collective-permute-start | bytes 1179656 | tf_op jit(solution)/shard_map/ppermute | solution.py:276
  161.1 18.0 %copy-start.2 = (bf16[6,384,512]{2,1,0:T(8,128)(2,1)S(1)}, bf16[6,384,512]{2,1,0:T(8,128)(2,1)}, u32[]{:S(2)}) copy-start(bf16[6,384,512]{2,1,0:T(8,128)(2,1)} %copy-done.1) | copy-start | bytes 7077892
  179.0 31.5 %collective-permute-start.5 = (bf16[4,4,2,2,8,1024]{5,4,3,2,1,0:T(8,128)(2,1)S(1)}, bf16[4,4,2,2,8,1024]{5,4,3,2,1,0:T(8,128)(2,1)}, u32[]{:S(2)}, u32[]{:S(2)}) collective-permute-start(bf16[4,4,2,2,8,1024]{5,4,3,2,1,0:T(8,128)(2,1)S(1)} %dynamic-slice_bitcast_fusion), channel_id=1, source_target_pairs={{0,8},{8,0},{16,24},{24,16},{1,9},{9,1},{17,25},{25,17},{2,10},{10... | collective-permute-start | bytes 3145736 | tf_op jit(solution)/shard_map/ppermute | solution.py:276
  183.9 18.2 %collective-permute-start.12 = (bf16[6,96,512]{2,1,0:T(8,128)(2,1)}, bf16[6,96,512]{2,1,0:T(8,128)(2,1)}, u32[]{:S(2)}, u32[]{:S(2)}) collective-permute-start(bf16[6,96,512]{2,1,0:T(8,128)(2,1)} %dynamic-slice_bitcast_fusion.1), channel_id=1, source_target_pairs={{0,2},{1,3},{2,4},{3,5},{4,6},{5,7},{6,0},{7,1},{8,10},{9,11},{10,... | collective-permute-start | bytes 1769480 | tf_op jit(solution)/shard_map/ppermute | solution.py:276
  186.3 24.2 %collective-permute-start.16 = (bf16[6,64,512]{2,1,0:T(8,128)(2,1)}, bf16[6,64,512]{2,1,0:T(8,128)(2,1)}, u32[]{:S(2)}, u32[]{:S(2)}) collective-permute-start(bf16[6,64,512]{2,1,0:T(8,128)(2,1)} %fusion.10), channel_id=1, source_target_pairs={{0,2},{1,3},{2,4},{3,5},{4,6},{5,7},{6,0},{7,1},{8,10},{9,11},{10,... | collective-permute-start | bytes 1179656 | tf_op jit(solution)/shard_map/ppermute | solution.py:276
  204.4 18.8 %collective-permute-start.13 = (bf16[6,96,512]{2,1,0:T(8,128)(2,1)}, bf16[6,96,512]{2,1,0:T(8,128)(2,1)}, u32[]{:S(2)}, u32[]{:S(2)}) collective-permute-start(bf16[6,96,512]{2,1,0:T(8,128)(2,1)} %fusion.3), channel_id=1, source_target_pairs={{0,2},{1,3},{2,4},{3,5},{4,6},{5,7},{6,0},{7,1},{8,10},{9,11},{10,... | collective-permute-start | bytes 1769480 | tf_op jit(solution)/shard_map/ppermute | solution.py:276
  212.2 19.3 %collective-permute-start.6 = (bf16[4,4,2,8,1024]{4,3,2,1,0:T(8,128)(2,1)S(1)}, bf16[4,4,2,8,1024]{4,3,2,1,0:T(8,128)(2,1)S(1)}, u32[]{:S(2)}, u32[]{:S(2)}) collective-permute-start(bf16[4,4,2,8,1024]{4,3,2,1,0:T(8,128)(2,1)S(1)} %dynamic-slice_bitcast_fusion.3), channel_id=1, source_target_pairs={{0,16},{8,24},{16,0},{24,8},{1,17},{9,25},{17,1},{25,9},{2,18},{10... | collective-permute-start | bytes 1572872 | tf_op jit(solution)/shard_map/ppermute | solution.py:276
  215.0 16.5 %collective-permute-start.17 = (bf16[6,64,512]{2,1,0:T(8,128)(2,1)S(1)}, bf16[6,64,512]{2,1,0:T(8,128)(2,1)S(1)}, u32[]{:S(2)}, u32[]{:S(2)}) collective-permute-start(bf16[6,64,512]{2,1,0:T(8,128)(2,1)S(1)} %fusion.9), channel_id=1, source_target_pairs={{0,2},{1,3},{2,4},{3,5},{4,6},{5,7},{6,0},{7,1},{8,10},{9,11},{10,... | collective-permute-start | bytes 1179656 | tf_op jit(solution)/shard_map/ppermute | solution.py:276
  224.6 19.2 %collective-permute-start.14 = (bf16[6,96,512]{2,1,0:T(8,128)(2,1)S(1)}, bf16[6,96,512]{2,1,0:T(8,128)(2,1)S(1)}, u32[]{:S(2)}, u32[]{:S(2)}) collective-permute-start(bf16[6,96,512]{2,1,0:T(8,128)(2,1)S(1)} %fusion.2), channel_id=1, source_target_pairs={{0,2},{1,3},{2,4},{3,5},{4,6},{5,7},{6,0},{7,1},{8,10},{9,11},{10,... | collective-permute-start | bytes 1769480 | tf_op jit(solution)/shard_map/ppermute | solution.py:276
  231.7 13.4 %copy-start.15 = (bf16[6,96,512]{2,1,0:T(8,128)(2,1)S(1)}, bf16[6,96,512]{2,1,0:T(8,128)(2,1)}, u32[]{:S(2)}) copy-start(bf16[6,96,512]{2,1,0:T(8,128)(2,1)} %fusion.4) | copy-start | bytes 1769476
  231.7 13.2 %collective-permute-start.7 = (bf16[4,4,8,1024]{3,2,1,0:T(8,128)(2,1)S(1)}, bf16[4,4,8,1024]{3,2,1,0:T(8,128)(2,1)S(1)}, u32[]{:S(2)}, u32[]{:S(2)}) collective-permute-start(bf16[4,4,8,1024]{3,2,1,0:T(8,128)(2,1)S(1)} %dynamic-slice_bitcast_fusion.5), channel_id=1, source_target_pairs={{0,1},{1,0},{2,3},{3,2},{4,5},{5,4},{6,7},{7,6},{8,9},{9,8},{10,11... | collective-permute-start | bytes 786440 | tf_op jit(solution)/shard_map/ppermute | solution.py:276
  245.1 6.1 %collective-permute-start.8 = (bf16[4,8,1024]{2,1,0:T(8,128)(2,1)S(1)}, bf16[4,8,1024]{2,1,0:T(8,128)(2,1)S(1)}, u32[]{:S(2)}, u32[]{:S(2)}) collective-permute-start(bf16[4,8,1024]{2,1,0:T(8,128)(2,1)S(1)} %dynamic-slice_bitcast_fusion.6), channel_id=1, source_target_pairs={{0,2},{1,3},{2,4},{3,5},{4,6},{5,7},{6,0},{7,1},{8,10},{9,11},{10,... | collective-permute-start | bytes 196616 | tf_op jit(solution)/shard_map/ppermute | solution.py:276
  249.1 3.3 %collective-permute-start.18 = (f32[16,256]{1,0:T(8,128)S(1)}, f32[16,256]{1,0:T(8,128)S(1)}, u32[]{:S(2)}, u32[]{:S(2)}) collective-permute-start(f32[16,256]{1,0:T(8,128)S(1)} %bitcast.118), channel_id=1, source_target_pairs={{0,8},{8,0},{16,24},{24,16},{1,9},{9,1},{17,25},{25,17},{2,10},{10... | collective-permute-start | bytes 49160 | tf_op jit(solution)/shard_map/ppermute | solution.py:288
  249.2 3.8 %collective-permute-start.19 = (f32[16,256]{1,0:T(8,128)S(1)}, f32[16,256]{1,0:T(8,128)S(1)}, u32[]{:S(2)}, u32[]{:S(2)}) collective-permute-start(f32[16,256]{1,0:T(8,128)S(1)} %bitcast.119), channel_id=1, source_target_pairs={{0,16},{8,24},{16,0},{24,8},{1,17},{9,25},{17,1},{25,9},{2,18},{10... | collective-permute-start | bytes 49160 | tf_op jit(solution)/shard_map/ppermute | solution.py:288
  250.7 3.2 %collective-permute-start.20 = (f32[16,256]{1,0:T(8,128)S(1)}, f32[16,256]{1,0:T(8,128)S(1)}, u32[]{:S(2)}, u32[]{:S(2)}) collective-permute-start(f32[16,256]{1,0:T(8,128)S(1)} %bitcast.120), channel_id=1, source_target_pairs={{0,24},{8,16},{16,8},{24,0},{1,25},{9,17},{17,9},{25,1},{2,26},{10... | collective-permute-start | bytes 49160 | tf_op jit(solution)/shard_map/ppermute | solution.py:288
  251.2 10.9 %collective-permute-start.9 = (bf16[4,8,1024]{2,1,0:T(8,128)(2,1)S(1)}, bf16[4,8,1024]{2,1,0:T(8,128)(2,1)S(1)}, u32[]{:S(2)}, u32[]{:S(2)}) collective-permute-start(bf16[4,8,1024]{2,1,0:T(8,128)(2,1)S(1)} %fusion.18), channel_id=1, source_target_pairs={{0,2},{1,3},{2,4},{3,5},{4,6},{5,7},{6,0},{7,1},{8,10},{9,11},{10,... | collective-permute-start | bytes 196616 | tf_op jit(solution)/shard_map/ppermute | solution.py:276
  253.9 3.8 %collective-permute-start.21 = (f32[16,256]{1,0:T(8,128)S(1)}, f32[16,256]{1,0:T(8,128)S(1)}, u32[]{:S(2)}, u32[]{:S(2)}) collective-permute-start(f32[16,256]{1,0:T(8,128)S(1)} %add_add_fusion), channel_id=1, source_target_pairs={{0,1},{1,0},{2,3},{3,2},{4,5},{5,4},{6,7},{7,6},{8,9},{9,8},{10,11... | collective-permute-start | bytes 49160 | tf_op jit(solution)/shard_map/ppermute | solution.py:288
  257.7 5.0 %collective-permute-start.22 = (f32[16,256]{1,0:T(8,128)S(1)}, f32[16,256]{1,0:T(8,128)S(1)}, u32[]{:S(2)}, u32[]{:S(2)}) collective-permute-start(f32[16,256]{1,0:T(8,128)S(1)} %add.440), channel_id=1, source_target_pairs={{0,2},{1,3},{2,0},{3,1},{4,6},{5,7},{6,4},{7,5},{8,10},{9,11},{10,... | collective-permute-start | bytes 49160 | tf_op jit(solution)/shard_map/ppermute | solution.py:288
  259.0 4.9 %collective-permute-start.23 = (f32[16,256]{1,0:T(8,128)S(1)}, f32[16,256]{1,0:T(8,128)S(1)}, u32[]{:S(2)}, u32[]{:S(2)}) collective-permute-start(f32[16,256]{1,0:T(8,128)S(1)} %add.440), channel_id=1, source_target_pairs={{0,4},{1,5},{2,6},{3,7},{4,0},{5,1},{6,2},{7,3},{8,12},{9,13},{10,... | collective-permute-start | bytes 49160 | tf_op jit(solution)/shard_map/ppermute | solution.py:288
  262.1 5.5 %collective-permute-start.24 = (f32[16,256]{1,0:T(8,128)S(1)}, f32[16,256]{1,0:T(8,128)S(1)}, u32[]{:S(2)}, u32[]{:S(2)}) collective-permute-start(f32[16,256]{1,0:T(8,128)S(1)} %add.440), channel_id=1, source_target_pairs={{0,6},{1,7},{2,4},{3,5},{4,2},{5,3},{6,0},{7,1},{8,14},{9,15},{10,... | collective-permute-start | bytes 49160 | tf_op jit(solution)/shard_map/ppermute | solution.py:288
  262.1 7.7 %collective-permute-start.10 = (bf16[4,8,1024]{2,1,0:T(8,128)(2,1)S(1)}, bf16[4,8,1024]{2,1,0:T(8,128)(2,1)S(1)}, u32[]{:S(2)}, u32[]{:S(2)}) collective-permute-start(bf16[4,8,1024]{2,1,0:T(8,128)(2,1)S(1)} %fusion.17), channel_id=1, source_target_pairs={{0,2},{1,3},{2,4},{3,5},{4,6},{5,7},{6,0},{7,1},{8,10},{9,11},{10,... | collective-permute-start | bytes 196616 | tf_op jit(solution)/shard_map/ppermute | solution.py:276
  (10 other events, 26.3 us)
